TPU v7x, 32 devices: a whole 2x2x4 slice. The times are simulated.
32 devices in a mesh: rows: 4 (over z), cols: 4 (over y, x), slab: 2 (over core).
Axes of the slice: x: 2, y: 2, z: 4, core: 2. Of those that a mesh axis runs over, the one named last changes fastest.
Arguments:
- density_blocks: bfloat16 [2048, 4096], P(('rows', 'cols', 'slab')), may hold values from -6 to 6
- block_owner: int32 [2048, 1], P(('rows', 'cols', 'slab')), may hold values from 0 to 31; in each aligned block of 64 rows (0 to 63, 64 to 127, ...) at most 4 rows name the same one
- block_plane: int32 [2048], P(('rows', 'cols', 'slab')), may hold values from 0 to 7
- block_segment: int32 [2048], P(('rows', 'cols', 'slab')), may hold values from 0 to 7
- block_kinds: int32 [2048, 2], P(('rows', 'cols', 'slab')), may hold values from 0 to 3
- basis: bfloat16 [4, 64, 4096], replicated, may hold values from -1.015625 to 1.015625
- ext_potential: float32 [256, 4096], P(('rows', 'cols', 'slab')), may hold values from -6 to 6
Outputs:
- density: float32 [256, 4096], P(('rows', 'cols', 'slab'))
- matrix_blocks: bfloat16 [2048, 4096], P(('rows', 'cols', 'slab'))
Inputs may be any that keep to these rules, and one draw needn't show every extreme that they name: `block_owner`: among the blocks of one device no owner is named more than 4 times; some owner is named exactly 4 times.
All inputs are finite; a program needn't handle non-finite values.
Results may differ from a plain program's by a relative error of at most 0.0095.
Values may be sent and summed in bfloat16 or wider, within the bound.
A program may use at most 128 MiB of HBM per device.

v0:
```python
import jax
import jax.numpy as jnp
from jax import lax
from jax.sharding import PartitionSpec as P

CZB = 8
SEGW = 512


def shifted(x, axis, by):
    size = lax.axis_size(axis)
    return lax.ppermute(x, axis, [(i, (i + by) % size) for i in range(size)])


def pick_basis(kind_ids, basis):
    kind_hot = (kind_ids[:, None] == jnp.arange(basis.shape[0], dtype=jnp.int32)[None, :]).astype(
        jnp.bfloat16
    )
    return jnp.einsum("bk,knc->bnc", kind_hot, basis, preferred_element_type=jnp.float32).astype(
        jnp.bfloat16
    )


def placement(meta_batch, czb_count, zext, segs):
    offsets = jnp.arange(czb_count, dtype=jnp.int32)
    plane_hot = (
        meta_batch[:, 0][:, None, None] + offsets[None, :, None]
        == jnp.arange(zext, dtype=jnp.int32)[None, None, :]
    ).astype(jnp.float32)
    seg_hot = (meta_batch[:, 1][:, None] == jnp.arange(segs, dtype=jnp.int32)[None, :]).astype(
        jnp.float32
    )
    place = plane_hot[:, :, :, None] * seg_hot[:, None, None, :]
    return place.reshape(meta_batch.shape[0] * czb_count, zext * segs)


def local(
    density_blocks, block_owner, block_plane, block_segment, block_kinds, basis, ext_potential
):
    device_count = lax.axis_size(("rows", "cols", "slab"))
    block_count = density_blocks.shape[0]
    capacity = max(2, (2 * block_count + device_count - 1) // device_count)
    width = basis.shape[1]
    cube_cells = basis.shape[2]
    zplanes = ext_potential.shape[0]
    segs = ext_potential.shape[1] // SEGW
    owner_index = block_owner[:, 0]
    one_hot = (owner_index[:, None] == jnp.arange(device_count, dtype=jnp.int32)[None, :]).astype(
        jnp.int32
    )
    rank_within = jnp.sum((jnp.cumsum(one_hot, axis=0) - one_hot) * one_hot, axis=1)
    slot_index = owner_index * capacity + rank_within
    block_meta = jnp.stack(
        [block_plane, block_segment, block_kinds[:, 0], block_kinds[:, 1]], axis=1
    )
    slot_total = device_count * capacity
    send_blocks = (
        jnp.zeros((slot_total, density_blocks.shape[1]), jnp.bfloat16)
        .at[slot_index]
        .set(density_blocks)
    )
    send_meta = jnp.zeros((slot_total, 4), jnp.int32).at[slot_index].set(block_meta)
    got_blocks, got_meta = (
        lax.all_to_all(
            send_blocks, ("rows", "cols", "slab"), split_axis=0, concat_axis=0, tiled=True
        ),
        lax.all_to_all(
            send_meta, ("rows", "cols", "slab"), split_axis=0, concat_axis=0, tiled=True
        ),
    )
    per_batch = min(32, slot_total)
    batch_count = slot_total // per_batch
    meta_batches = got_meta.reshape(batch_count, per_batch, 4)
    block_batches = got_blocks.reshape(batch_count, per_batch, width, width)
    zext = zplanes + CZB - 1
    extended_rows = zext * segs

    def deposit(grid_rows, batch_item):
        block_batch, meta_batch = batch_item
        row_basis = pick_basis(meta_batch[:, 2], basis)
        col_basis = pick_basis(meta_batch[:, 3], basis)
        half_product = jnp.einsum(
            "bmn,bnc->bmc", block_batch, col_basis, preferred_element_type=jnp.float32
        ).astype(jnp.bfloat16)
        product_tile = jnp.einsum(
            "bmc,bmc->bc", row_basis, half_product, preferred_element_type=jnp.float32
        )
        place = placement(meta_batch, CZB, zext, segs)
        added = jnp.einsum(
            "rz,rw->zw", place, product_tile.reshape(-1, SEGW), precision=lax.Precision.HIGHEST
        )
        return (grid_rows + added, None)

    grid_rows, _ = lax.scan(
        deposit, jnp.zeros((extended_rows, SEGW), jnp.float32), (block_batches, meta_batches)
    )
    owned_rows = zplanes * segs
    rim_rows = (CZB - 1) * segs
    arrived = shifted(grid_rows[owned_rows:], ("rows", "cols", "slab"), 1)
    owned = grid_rows[:owned_rows]
    owned = jnp.concatenate([owned[:rim_rows] + arrived, owned[rim_rows:]], axis=0)
    density = owned.reshape(zplanes, -1)
    potential = (ext_potential + 0.5 * density).reshape(owned_rows, SEGW)
    upper_rim = shifted(potential[:rim_rows], ("rows", "cols", "slab"), -1)
    potential_ext = jnp.concatenate([potential, upper_rim], axis=0)

    def integrate(carry, meta_batch):
        row_basis = pick_basis(meta_batch[:, 2], basis)
        col_basis = pick_basis(meta_batch[:, 3], basis)
        place = placement(meta_batch, CZB, zext, segs)
        pot_tile = jnp.einsum(
            "rz,zw->rw", place, potential_ext, precision=lax.Precision.HIGHEST
        ).reshape(per_batch, cube_cells)
        weighted = (row_basis.astype(jnp.float32) * pot_tile[:, None, :]).astype(jnp.bfloat16)
        matrix_tile = jnp.einsum(
            "bmc,bnc->bmn", weighted, col_basis, preferred_element_type=jnp.float32
        ).astype(jnp.bfloat16)
        return (carry, matrix_tile.reshape(per_batch, width * width))

    _, matrix_tiles = lax.scan(integrate, jnp.zeros((), jnp.float32), meta_batches)
    matrix_slots = matrix_tiles.reshape(slot_total, width * width)
    returned = lax.all_to_all(
        matrix_slots, ("rows", "cols", "slab"), split_axis=0, concat_axis=0, tiled=True
    )
    matrix_blocks = returned[slot_index]
    return (density, matrix_blocks)


def solution(mesh):
    placed = (
        P(("rows", "cols", "slab"), None),
        P(("rows", "cols", "slab"), None),
        P(("rows", "cols", "slab")),
        P(("rows", "cols", "slab")),
        P(("rows", "cols", "slab"), None),
        P(),
        P(("rows", "cols", "slab"), None),
    )
    return jax.shard_map(
        local,
        mesh=mesh,
        in_specs=placed,
        out_specs=(P(("rows", "cols", "slab"), None), P(("rows", "cols", "slab"), None)),
        check_vma=False,
    )
```

profile of v0, /device:TPU:0, one launch (start us, length us, event | category | flops | bytes accessed | tf_op | source)
XLA Modules:
  0.0 637.2 jit_solution(682111318484399651)
XLA Ops:
  5.5 7.3 %all-to-all-start = ((s32[32,4,4]{1,2,0:T(4,128)}), s32[32,4,4]{1,2,0:T(4,128)S(1)}, u32[]{:S(2)}, u32[]{:S(2)}) async-start(s32[32,4,4]{1,2,0:T(4,128)} %copy.17), calls=%async_computation | async-start | bytes 131072 | tf_op jit(solution)/shard_map/all_to_all | solution.py:67
  12.8 2.2 scatter_custom_fusion.1
  16.1 4.0 all-to-all-done
  20.2 2.6 all-to-all-start.1
  22.8 3.2 copy.20
  26.2 22.9 %all-to-all-done.1 = bf16[32,4,4096]{2,1,0:T(4,128)(2,1)S(1)} async-done(((bf16[32,4,4096]{2,1,0:T(4,128)(2,1)}), bf16[32,4,4096]{2,1,0:T(4,128)(2,1)S(1)}, u32[]{:S(2)}, u32[]{:S(2)}) %all-to-all-start.1) | async-done | bytes 1048608 | tf_op jit(solution)/shard_map/all_to_all | solution.py:64
  49.0 2.7 reshape.153
  51.7 320.8 %while.22 = (s32[]{:T(128)}, f32[120,512]{1,0:T(8,128)S(1)}, s32[4,32,4]{1,2,0:T(4,128)S(1)}, bf16[4,64,4096]{2,0,1:T(4,128)(2,1)S(1)}, bf16[4,32,64,64]{3,2,1,0:T(8,128)(2,1)}, /*index=5*/s32[]{:T(128)}, s32[]{:T(128)}) while((s32[]{:T(128)}, f32[120,512]{1,0:T(8,128)S(1)}, s32[4,32,4]{1,2,0:T(4,128)S(1)}, ...), condition=%wide.region_5.6_spmd.clone, body=%wide.region_4.5_spmd.clone.sunk | while | flops 1455454720 | bytes 108500056 | solution.py:94
  51.9 13.1 %bitcast_convert_fusion.2 = f32[32,4096,64]{1,0,2:T(8,128)} fusion(bf16[4,64,4096]{2,0,1:T(4,128)(2,1)S(1)} %get-tuple-element.219, s32[32]{0:T(128)S(1)} %get-tuple-element.200), kind=kOutput, calls=%fused_computation.28.clone.1 | convolution fusion | flops 83886208 | bytes 35651712 | tf_op jit(solution)/shard_map/while/body/eval_jaxpr/bk,knc->bnc/dot_general | solution.py:19
  65.0 8.1 %convolution_convert_fusion.5 = bf16[32,64,4096]{2,0,1:T(8,128)(2,1)} fusion(bf16[4,64,4096]{2,0,1:T(4,128)(2,1)S(1)} %get-tuple-element.219, s32[32]{0:T(128)S(1)} %get-tuple-element.201), kind=kOutput, calls=%fused_computation.31.clone.1 | convolution fusion | flops 75497600 | bytes 18874496 | tf_op jit(solution)/shard_map/while/body/eval_jaxpr/bk,knc->bnc/dot_general | solution.py:19
  73.2 50.1 %multiply_reduce_fusion.2 = f32[32,4096]{1,0:T(8,128)S(1)} fusion(f32[32,4096,64]{1,0,2:T(8,128)} %bitcast_convert_fusion.2, bf16[32,64,4096]{2,0,1:T(8,128)(2,1)} %convolution_convert_fusion.5, bf16[4,32,64,64]{3,2,1,0:T(8,128)(2,1)} %get-tuple-element.220, s32[]{:T(128)} %get-tuple-element.209), kind=kOutput, calls=%fused_computation.27.clone.1 | convolution fusion | flops 1107165184 | bytes 51380736 | tf_op jit(solution)/shard_map/while/body/eval_jaxpr/bmn,bnc->bmc/dot_general | solution.py:82
  123.5 1.6 broadcast_multiply_fusion.5
  125.1 2.6 mul.109
  128.3 13.1 %bitcast_convert_fusion.2 = f32[32,4096,64]{1,0,2:T(8,128)} fusion(bf16[4,64,4096]{2,0,1:T(4,128)(2,1)S(1)} %get-tuple-element.219, s32[32]{0:T(128)S(1)} %get-tuple-element.200), kind=kOutput, calls=%fused_computation.28.clone.1 | convolution fusion | flops 83886208 | bytes 35651712 | tf_op jit(solution)/shard_map/while/body/eval_jaxpr/bk,knc->bnc/dot_general | solution.py:19
  141.4 8.1 %convolution_convert_fusion.5 = bf16[32,64,4096]{2,0,1:T(8,128)(2,1)} fusion(bf16[4,64,4096]{2,0,1:T(4,128)(2,1)S(1)} %get-tuple-element.219, s32[32]{0:T(128)S(1)} %get-tuple-element.201), kind=kOutput, calls=%fused_computation.31.clone.1 | convolution fusion | flops 75497600 | bytes 18874496 | tf_op jit(solution)/shard_map/while/body/eval_jaxpr/bk,knc->bnc/dot_general | solution.py:19
  149.5 50.1 %multiply_reduce_fusion.2 = f32[32,4096]{1,0:T(8,128)S(1)} fusion(f32[32,4096,64]{1,0,2:T(8,128)} %bitcast_convert_fusion.2, bf16[32,64,4096]{2,0,1:T(8,128)(2,1)} %convolution_convert_fusion.5, bf16[4,32,64,64]{3,2,1,0:T(8,128)(2,1)} %get-tuple-element.220, s32[]{:T(128)} %get-tuple-element.209), kind=kOutput, calls=%fused_computation.27.clone.1 | convolution fusion | flops 1107165184 | bytes 51380736 | tf_op jit(solution)/shard_map/while/body/eval_jaxpr/bmn,bnc->bmc/dot_general | solution.py:82
  201.5 2.6 mul.109
  204.6 13.1 %bitcast_convert_fusion.2 = f32[32,4096,64]{1,0,2:T(8,128)} fusion(bf16[4,64,4096]{2,0,1:T(4,128)(2,1)S(1)} %get-tuple-element.219, s32[32]{0:T(128)S(1)} %get-tuple-element.200), kind=kOutput, calls=%fused_computation.28.clone.1 | convolution fusion | flops 83886208 | bytes 35651712 | tf_op jit(solution)/shard_map/while/body/eval_jaxpr/bk,knc->bnc/dot_general | solution.py:19
  217.7 8.1 %convolution_convert_fusion.5 = bf16[32,64,4096]{2,0,1:T(8,128)(2,1)} fusion(bf16[4,64,4096]{2,0,1:T(4,128)(2,1)S(1)} %get-tuple-element.219, s32[32]{0:T(128)S(1)} %get-tuple-element.201), kind=kOutput, calls=%fused_computation.31.clone.1 | convolution fusion | flops 75497600 | bytes 18874496 | tf_op jit(solution)/shard_map/while/body/eval_jaxpr/bk,knc->bnc/dot_general | solution.py:19
  225.8 50.1 %multiply_reduce_fusion.2 = f32[32,4096]{1,0:T(8,128)S(1)} fusion(f32[32,4096,64]{1,0,2:T(8,128)} %bitcast_convert_fusion.2, bf16[32,64,4096]{2,0,1:T(8,128)(2,1)} %convolution_convert_fusion.5, bf16[4,32,64,64]{3,2,1,0:T(8,128)(2,1)} %get-tuple-element.220, s32[]{:T(128)} %get-tuple-element.209), kind=kOutput, calls=%fused_computation.27.clone.1 | convolution fusion | flops 1107165184 | bytes 51380736 | tf_op jit(solution)/shard_map/while/body/eval_jaxpr/bmn,bnc->bmc/dot_general | solution.py:82
  277.8 2.6 mul.109
  280.9 13.1 %bitcast_convert_fusion.2 = f32[32,4096,64]{1,0,2:T(8,128)} fusion(bf16[4,64,4096]{2,0,1:T(4,128)(2,1)S(1)} %get-tuple-element.219, s32[32]{0:T(128)S(1)} %get-tuple-element.200), kind=kOutput, calls=%fused_computation.28.clone.1 | convolution fusion | flops 83886208 | bytes 35651712 | tf_op jit(solution)/shard_map/while/body/eval_jaxpr/bk,knc->bnc/dot_general | solution.py:19
  294.1 8.1 %convolution_convert_fusion.5 = bf16[32,64,4096]{2,0,1:T(8,128)(2,1)} fusion(bf16[4,64,4096]{2,0,1:T(4,128)(2,1)S(1)} %get-tuple-element.219, s32[32]{0:T(128)S(1)} %get-tuple-element.201), kind=kOutput, calls=%fused_computation.31.clone.1 | convolution fusion | flops 75497600 | bytes 18874496 | tf_op jit(solution)/shard_map/while/body/eval_jaxpr/bk,knc->bnc/dot_general | solution.py:19
  302.2 50.1 %multiply_reduce_fusion.2 = f32[32,4096]{1,0:T(8,128)S(1)} fusion(f32[32,4096,64]{1,0,2:T(8,128)} %bitcast_convert_fusion.2, bf16[32,64,4096]{2,0,1:T(8,128)(2,1)} %convolution_convert_fusion.5, bf16[4,32,64,64]{3,2,1,0:T(8,128)(2,1)} %get-tuple-element.220, s32[]{:T(128)} %get-tuple-element.209), kind=kOutput, calls=%fused_computation.27.clone.1 | convolution fusion | flops 1107165184 | bytes 51380736 | tf_op jit(solution)/shard_map/while/body/eval_jaxpr/bmn,bnc->bmc/dot_general | solution.py:82
  354.2 2.6 mul.109
  372.6 7.8 %collective-permute-done = f32[56,512]{1,0:T(8,128)S(1)} collective-permute-done((f32[56,512]{1,0:T(8,128)S(1)}, f32[56,512]{1,0:T(8,128)S(1)}, u32[]{:S(2)}, u32[]{:S(2)}) %collective-permute-start) | collective-permute-done | bytes 114720 | tf_op jit(solution)/shard_map/ppermute | solution.py:12
  380.7 2.3 collective-permute-done.1
  383.0 217.8 %while.21 = (s32[]{:T(128)}, bf16[4,32,4096]{2,1,0:T(8,128)(2,1)}, s32[4,32,4]{1,2,0:T(4,128)S(1)}, bf16[4,64,4096]{2,0,1:T(4,128)(2,1)S(1)}, f32[120,512]{1,0:T(8,128)S(1)}, /*index=5*/s32[]{:T(128)}) while((s32[]{:T(128)}, bf16[4,32,4096]{2,1,0:T(8,128)(2,1)}, s32[4,32,4]{1,2,0:T(4,128)S(1)}, bf16[4,64,4096]{2,0,1:T(4,128)(2,1)S(1)}, ...), condition=%wide.region_7.8_spmd, body=%wide.region_6.7_spmd.sunk | while | flops 1438816768 | bytes 75486280 | solution.py:120
  384.8 2.6 mul.104
  388.2 8.1 %multiply_convert_fusion.2 = bf16[32,64,4096]{2,0,1:T(8,128)(2,1)} fusion(f32[32,4096]{1,0:T(8,128)S(1)} %mul.105, bf16[4,64,4096]{2,0,1:T(4,128)(2,1)S(1)} %get-tuple-element.238, s32[32]{0:T(128)S(1)} %get-tuple-element.192), kind=kOutput, calls=%fused_computation.3.clone.1 | convolution fusion | flops 100663424 | bytes 19398784 | tf_op jit(solution)/shard_map/while/body/eval_jaxpr/bk,knc->bnc/dot_general | solution.py:19
  396.3 8.1 %convolution_convert_fusion.4 = bf16[32,64,4096]{2,0,1:T(8,128)(2,1)} fusion(bf16[4,64,4096]{2,0,1:T(4,128)(2,1)S(1)} %get-tuple-element.238, s32[32]{0:T(128)S(1)} %get-tuple-element.189), kind=kOutput, calls=%fused_computation.7.clone.1 | convolution fusion | flops 75497600 | bytes 18874496 | tf_op jit(solution)/shard_map/while/body/eval_jaxpr/bk,knc->bnc/dot_general | solution.py:19
  404.4 31.9 %fusion.79 = bf16[32,64,64]{2,1,0:T(8,128)(2,1)S(1)} fusion(bf16[32,64,4096]{2,0,1:T(8,128)(2,1)} %convolution_convert_fusion.4, bf16[32,64,4096]{2,0,1:T(8,128)(2,1)} %multiply_convert_fusion.2), kind=kOutput, calls=%fused_computation.8.clone.1 | convolution fusion | flops 1073872896 | bytes 33816576 | tf_op jit(solution)/shard_map/while/body/eval_jaxpr/bmc,bnc->bmn/dot_general | solution.py:115
  439.2 2.6 mul.104
  442.6 8.1 %multiply_convert_fusion.2 = bf16[32,64,4096]{2,0,1:T(8,128)(2,1)} fusion(f32[32,4096]{1,0:T(8,128)S(1)} %mul.105, bf16[4,64,4096]{2,0,1:T(4,128)(2,1)S(1)} %get-tuple-element.238, s32[32]{0:T(128)S(1)} %get-tuple-element.192), kind=kOutput, calls=%fused_computation.3.clone.1 | convolution fusion | flops 100663424 | bytes 19398784 | tf_op jit(solution)/shard_map/while/body/eval_jaxpr/bk,knc->bnc/dot_general | solution.py:19
  450.7 8.1 %convolution_convert_fusion.4 = bf16[32,64,4096]{2,0,1:T(8,128)(2,1)} fusion(bf16[4,64,4096]{2,0,1:T(4,128)(2,1)S(1)} %get-tuple-element.238, s32[32]{0:T(128)S(1)} %get-tuple-element.189), kind=kOutput, calls=%fused_computation.7.clone.1 | convolution fusion | flops 75497600 | bytes 18874496 | tf_op jit(solution)/shard_map/while/body/eval_jaxpr/bk,knc->bnc/dot_general | solution.py:19
  458.8 31.9 %fusion.79 = bf16[32,64,64]{2,1,0:T(8,128)(2,1)S(1)} fusion(bf16[32,64,4096]{2,0,1:T(8,128)(2,1)} %convolution_convert_fusion.4, bf16[32,64,4096]{2,0,1:T(8,128)(2,1)} %multiply_convert_fusion.2), kind=kOutput, calls=%fused_computation.8.clone.1 | convolution fusion | flops 1073872896 | bytes 33816576 | tf_op jit(solution)/shard_map/while/body/eval_jaxpr/bmc,bnc->bmn/dot_general | solution.py:115
  493.7 2.6 mul.104
  497.1 8.1 %multiply_convert_fusion.2 = bf16[32,64,4096]{2,0,1:T(8,128)(2,1)} fusion(f32[32,4096]{1,0:T(8,128)S(1)} %mul.105, bf16[4,64,4096]{2,0,1:T(4,128)(2,1)S(1)} %get-tuple-element.238, s32[32]{0:T(128)S(1)} %get-tuple-element.192), kind=kOutput, calls=%fused_computation.3.clone.1 | convolution fusion | flops 100663424 | bytes 19398784 | tf_op jit(solution)/shard_map/while/body/eval_jaxpr/bk,knc->bnc/dot_general | solution.py:19
  505.2 8.1 %convolution_convert_fusion.4 = bf16[32,64,4096]{2,0,1:T(8,128)(2,1)} fusion(bf16[4,64,4096]{2,0,1:T(4,128)(2,1)S(1)} %get-tuple-element.238, s32[32]{0:T(128)S(1)} %get-tuple-element.189), kind=kOutput, calls=%fused_computation.7.clone.1 | convolution fusion | flops 75497600 | bytes 18874496 | tf_op jit(solution)/shard_map/while/body/eval_jaxpr/bk,knc->bnc/dot_general | solution.py:19
  513.3 31.9 %fusion.79 = bf16[32,64,64]{2,1,0:T(8,128)(2,1)S(1)} fusion(bf16[32,64,4096]{2,0,1:T(8,128)(2,1)} %convolution_convert_fusion.4, bf16[32,64,4096]{2,0,1:T(8,128)(2,1)} %multiply_convert_fusion.2), kind=kOutput, calls=%fused_computation.8.clone.1 | convolution fusion | flops 1073872896 | bytes 33816576 | tf_op jit(solution)/shard_map/while/body/eval_jaxpr/bmc,bnc->bmn/dot_general | solution.py:115
  548.1 2.6 mul.104
  551.5 8.1 %multiply_convert_fusion.2 = bf16[32,64,4096]{2,0,1:T(8,128)(2,1)} fusion(f32[32,4096]{1,0:T(8,128)S(1)} %mul.105, bf16[4,64,4096]{2,0,1:T(4,128)(2,1)S(1)} %get-tuple-element.238, s32[32]{0:T(128)S(1)} %get-tuple-element.192), kind=kOutput, calls=%fused_computation.3.clone.1 | convolution fusion | flops 100663424 | bytes 19398784 | tf_op jit(solution)/shard_map/while/body/eval_jaxpr/bk,knc->bnc/dot_general | solution.py:19
  559.6 8.1 %convolution_convert_fusion.4 = bf16[32,64,4096]{2,0,1:T(8,128)(2,1)} fusion(bf16[4,64,4096]{2,0,1:T(4,128)(2,1)S(1)} %get-tuple-element.238, s32[32]{0:T(128)S(1)} %get-tuple-element.189), kind=kOutput, calls=%fused_computation.7.clone.1 | convolution fusion | flops 75497600 | bytes 18874496 | tf_op jit(solution)/shard_map/while/body/eval_jaxpr/bk,knc->bnc/dot_general | solution.py:19
  567.7 31.9 %fusion.79 = bf16[32,64,64]{2,1,0:T(8,128)(2,1)S(1)} fusion(bf16[32,64,4096]{2,0,1:T(8,128)(2,1)} %convolution_convert_fusion.4, bf16[32,64,4096]{2,0,1:T(8,128)(2,1)} %multiply_convert_fusion.2), kind=kOutput, calls=%fused_computation.8.clone.1 | convolution fusion | flops 1073872896 | bytes 33816576 | tf_op jit(solution)/shard_map/while/body/eval_jaxpr/bmc,bnc->bmn/dot_general | solution.py:115
  600.8 2.2 all_to_all.24
  603.0 5.8 all-to-all-start.2
  608.9 26.2 %all-to-all-done.2 = bf16[32,4,4096]{2,1,0:T(4,128)(2,1)S(1)} async-done(((bf16[32,4,4096]{2,1,0:T(4,128)(2,1)}), bf16[32,4,4096]{2,1,0:T(4,128)(2,1)S(1)}, u32[]{:S(2)}, u32[]{:S(2)}) %all-to-all-start.2) | async-done | bytes 1048608 | tf_op jit(solution)/shard_map/all_to_all | solution.py:122
  635.3 1.7 gather_fusion
  (106 shorter events, 28.6 us)
Async XLA Ops:
  3.0 19.9 %copy-start.2 = (s32[64]{0:T(128)}, s32[64]{0:T(128)S(1)}, u32[]{:S(2)}) copy-start(s32[64]{0:T(128)S(1)} %fusion.36) | copy-start | bytes 772
  5.5 14.7 %all-to-all-start = ((s32[32,4,4]{1,2,0:T(4,128)}), s32[32,4,4]{1,2,0:T(4,128)S(1)}, u32[]{:S(2)}, u32[]{:S(2)}) async-start(s32[32,4,4]{1,2,0:T(4,128)} %copy.17), calls=%async_computation | async-start | bytes 131072 | tf_op jit(solution)/shard_map/all_to_all | solution.py:67
  20.2 28.9 %all-to-all-start.1 = ((bf16[32,4,4096]{2,1,0:T(4,128)(2,1)}), bf16[32,4,4096]{2,1,0:T(4,128)(2,1)S(1)}, u32[]{:S(2)}, u32[]{:S(2)}) async-start(bf16[32,4,4096]{2,1,0:T(4,128)(2,1)} %all_to_all.22), calls=%async_computation.1 | async-start | bytes 2097152 | tf_op jit(solution)/shard_map/all_to_all | solution.py:64
  51.7 328.7 %copy-start.1 = (f32[8,4096]{1,0:T(8,128)S(1)}, f32[8,4096]{1,0:T(8,128)}, u32[]{:S(2)}) copy-start(f32[8,4096]{1,0:T(8,128)} %param.17) | copy-start | bytes 393220
  372.5 7.9 %collective-permute-start = (f32[56,512]{1,0:T(8,128)S(1)}, f32[56,512]{1,0:T(8,128)S(1)}, u32[]{:S(2)}, u32[]{:S(2)}) collective-permute-start(f32[56,512]{1,0:T(8,128)S(1)} %slice.50), channel_id=1, source_target_pairs={{0,1},{1,2},{2,3},{3,4},{4,5},{5,6},{6,7},{7,8},{8,9},{9,10},{10,1... | collective-permute-start | bytes 344072 | tf_op jit(solution)/shard_map/ppermute | solution.py:12
  380.5 2.6 copy-start
  380.6 2.4 collective-permute-start.1
  383.0 225.8 %copy-start.3 = (s32[64]{0:T(128)S(1)}, s32[64]{0:T(128)}, u32[]{:S(2)}) copy-start(s32[64]{0:T(128)} %copy-done.2) | copy-start | bytes 772
  603.0 32.1 %all-to-all-start.2 = ((bf16[32,4,4096]{2,1,0:T(4,128)(2,1)}), bf16[32,4,4096]{2,1,0:T(4,128)(2,1)S(1)}, u32[]{:S(2)}, u32[]{:S(2)}) async-start(bf16[32,4,4096]{2,1,0:T(4,128)(2,1)} %all_to_all.24), calls=%async_computation.2 | async-start | bytes 2097152 | tf_op jit(solution)/shard_map/all_to_all | solution.py:122
where the time goes:
time: 642 us; the launch traced here: 637 us
  matrix products  482 us (75%)
  waiting for transfers between devices  63.2 us (10%)
  local copies, waits for them, and re-layouts  42.2 us (7%)
  other arithmetic  16.8 us (3%)
  starting transfers between devices  15.9 us (2%)
  loops' own time  15.9 us (2%)
    dot_general x4, matrix products, deposit(): jnp.einsum('bmn,bnc->bmc', block_batch, col_basis, preferred_element_type...  201 us
    dot_general x16, matrix products, pick_basis(): jnp.einsum('bk,knc->bnc', kind_hot, basis, preferred_element_type=jnp.flo...  150 us
    dot_general x4, matrix products, integrate(): jnp.einsum('bmc,bnc->bmn', weighted, col_basis, preferred_element_type=jn...  128 us
    all_to_all x1, waiting for transfers between devices, local(): lax.all_to_all(matrix_slots, ('rows', 'cols', 'slab'), split_axis=0, conc...  26.2 us
    all_to_all x1, waiting for transfers between devices, local(): lax.all_to_all(send_blocks, ('rows', 'cols', 'slab'), split_axis=0, conca...  22.9 us
    mul x8, local copies, waits for them, and re-layouts, placement(): place = plane_hot[:, :, :, None] * seg_hot[:, None, None, :]  21.1 us
    another operation x1, loops' own time, local(): lax.scan(deposit, jnp.zeros((extended_rows, SEGW), jnp.float32), (block_b...  15.7 us
    mul x8, other arithmetic, placement(): place = plane_hot[:, :, :, None] * seg_hot[:, None, None, :]  12.9 us
  transfers between devices with their start and end apart: 5, of which 5 were waited for; matrix products, arithmetic and copies ran while one was open for 1% of the time, Pallas kernels for 0%

commit v1 on v0

v1 whole, which is shorter than its diff:
```python
import functools

import jax
import jax.numpy as jnp
from jax import lax
from jax.experimental import pallas as pl
from jax.experimental.pallas import tpu as pltpu
from jax.sharding import PartitionSpec as P

CZB = 8
SEGW = 512
TILE = 256
AXES = ("rows", "cols", "slab")
VMEM = pl.BlockSpec(memory_space=pltpu.VMEM)
MESH = pl.DeviceIdType.MESH
SMEM = pl.BlockSpec(memory_space=pltpu.SMEM)


def deposit_kernel(width, count, kinds_ref, rows_ref, wide_ref, basis_ref, grid_ref, tiles_ref):
    halves = SEGW // TILE
    group = 8
    cells = basis_ref.shape[1]

    def column_tile(t, carry):
        i, h = t // halves, t % halves
        columns = pl.ds(pl.multiple_of(t * TILE, TILE), TILE)
        weights = basis_ref[:, columns]
        for g in range(count // group):
            lhs = wide_ref[pl.ds(g * group * width, group * width), :]
            half = jnp.dot(lhs, weights, preferred_element_type=jnp.float32)
            sums = []
            for b in range(group):
                kind = kinds_ref[g * group + b, 0]
                a = basis_ref[pl.ds(pl.multiple_of(kind * width, width), width), columns]
                product = a.astype(jnp.float32) * half[b * width : (b + 1) * width]
                sums.append(jnp.sum(product, axis=0, keepdims=True))
            row = pl.multiple_of(i * count + g * group, group)
            tiles_ref[pl.ds(row, group), pl.ds(pl.multiple_of(h * TILE, TILE), TILE)] = (
                jnp.concatenate(sums, axis=0)
            )
        return carry

    lax.fori_loop(0, cells // TILE, column_tile, 0)
    tiles = tiles_ref[...].astype(jnp.bfloat16)
    places = tiles.shape[0]
    chunk = 256

    def place(r, carry):
        base = pl.multiple_of(r * chunk, chunk)
        hot = rows_ref[...] == lax.broadcasted_iota(jnp.int32, (chunk, places), 0) + base
        hot = jnp.where(hot, 1.0, 0.0).astype(jnp.bfloat16)
        placed = jnp.dot(hot, tiles, preferred_element_type=jnp.float32).astype(jnp.bfloat16)
        for h in range(SEGW // TILE):
            grid_ref[h, pl.ds(base, chunk), :] = placed[:, h * TILE : (h + 1) * TILE]
        return carry

    lax.fori_loop(0, grid_ref.shape[1] // chunk, place, 0)


def integrate_kernel(
    width, count, kinds_ref, rows_ref, pot_ref, basis_ref, out_ref, tiles_ref, weighted_ref
):
    halves = SEGW // TILE
    group = 8
    cells = basis_ref.shape[1]
    places = tiles_ref.shape[0]
    grid_rows = pot_ref.shape[1]
    chunk = 256

    tiles_ref[...] = jnp.zeros_like(tiles_ref)

    def gather(r, carry):
        base = pl.multiple_of(r * chunk, chunk)
        hot = rows_ref[...] == lax.broadcasted_iota(jnp.int32, (places, chunk), 1) + base
        hot = jnp.where(hot, 1.0, 0.0).astype(jnp.bfloat16)
        for h in range(halves):
            tiles_ref[:, pl.ds(h * TILE, TILE)] += jnp.dot(
                hot, pot_ref[h, pl.ds(base, chunk), :], preferred_element_type=jnp.float32
            )
        return carry

    lax.fori_loop(0, grid_rows // chunk, gather, 0)

    def block_group(g, carry):
        for t in range(cells // TILE):
            i, h = t // halves, t % halves
            rows = pl.ds(pl.multiple_of(i * count + g * group, group), group)
            pots = tiles_ref[rows, pl.ds(h * TILE, TILE)]
            for b in range(group):
                kind = kinds_ref[g * group + b, 0]
                a = basis_ref[
                    pl.ds(pl.multiple_of(kind * width, width), width), pl.ds(t * TILE, TILE)
                ]
                weighted_ref[b * width : (b + 1) * width, t * TILE : (t + 1) * TILE] = (
                    a * jnp.broadcast_to(pots[b : b + 1], (width, TILE)).astype(jnp.bfloat16)
                )
        full = lax.dot_general(
            weighted_ref[...],
            basis_ref[...],
            (((1,), (1,)), ((), ())),
            preferred_element_type=jnp.float32,
        )
        for b in range(group):
            kind = kinds_ref[g * group + b, 1]
            mine = full[b * width : (b + 1) * width]
            picked = mine[:, :width]
            for k in range(1, basis_ref.shape[0] // width):
                picked = jnp.where(kind == k, mine[:, k * width : (k + 1) * width], picked)
            out_ref[pl.ds(pl.multiple_of((g * group + b) * width, width), width), :] = (
                picked.astype(jnp.bfloat16)
            )
        return carry

    lax.fori_loop(0, count // group, block_group, 0)


def peers_of(axis):
    size = lax.axis_size(axis)
    me = lax.axis_index(axis)
    return [lax.rem(me + o, size) for o in range(1, size)]


def greet():
    barrier = pltpu.get_barrier_semaphore()
    total = 0
    for axis in AXES:
        for peer in peers_of(axis):
            pl.semaphore_signal(barrier, inc=1, device_id={axis: peer}, device_id_type=MESH)
            total += 1
    pl.semaphore_wait(barrier, total)


def send(axis, peer, src, dst, sems, at):
    copy = pltpu.make_async_remote_copy(
        src_ref=src,
        dst_ref=dst,
        send_sem=sems.at[0, at],
        recv_sem=sems.at[1, at],
        device_id={axis: peer},
        device_id_type=MESH,
    )
    copy.start()
    return copy


class Exchange:
    def __init__(self, order, grid, pots, bufs, sems):
        self.order, self.grid, self.pots, self.sems = order, grid, pots, sems
        self.got1, self.sum1, self.got2, self.sum2, self.got3 = bufs
        self.r, self.c, self.s = (lax.axis_index(axis) for axis in AXES)
        self.sizes = {axis: lax.axis_size(axis) for axis in AXES}
        self.used = 0

    def next_sem(self):
        self.used += 1
        return self.used - 1

    def start1(self):
        (peer,) = peers_of("slab")
        self.copies = [
            send("slab", peer, self.grid.at[:, :, peer], self.got1, self.sems, self.next_sem())
        ]

    def wait(self):
        for copy in self.copies:
            copy.wait()

    def start2(self):
        self.wait()
        nr, nc = self.sizes["rows"], self.sizes["cols"]

        def add(n, carry):
            r, c = n // nc, n % nc
            self.sum1[r, c] = (
                self.grid[r, c, self.s].astype(jnp.float32) + self.got1[r, c].astype(jnp.float32)
            ).astype(jnp.bfloat16)
            return carry

        lax.fori_loop(0, nr * nc, add, 0)
        axis = self.order[0]
        self.copies = []
        for o, peer in enumerate(peers_of(axis)):
            src = self.sum1.at[peer] if axis == "rows" else self.sum1.at[:, peer]
            self.copies.append(send(axis, peer, src, self.got2.at[o], self.sems, self.next_sem()))

    def start3(self):
        self.wait()
        first, axis = self.order

        def add(n, carry):
            mine = self.sum1[self.r, n] if first == "rows" else self.sum1[n, self.c]
            total = mine.astype(jnp.float32)
            for o in range(self.sizes[first] - 1):
                total = total + self.got2[o, n].astype(jnp.float32)
            self.sum2[n] = total.astype(jnp.bfloat16)
            return carry

        lax.fori_loop(0, self.sizes[axis], add, 0)
        self.copies = []
        for o, peer in enumerate(peers_of(axis)):
            self.copies.append(
                send(axis, peer, self.sum2.at[peer], self.got3.at[o], self.sems, self.next_sem())
            )

    def finish(self):
        self.wait()
        axis = self.order[1]
        total = self.sum2[self.r if axis == "rows" else self.c].astype(jnp.float32)
        for o in range(self.sizes[axis] - 1):
            total = total + self.got3[o].astype(jnp.float32)
        return total

    def start4(self, potential):
        self.pots[self.r, self.c, self.s] = potential.astype(jnp.bfloat16)
        axis = self.order[1]
        mine = self.pots.at[self.r, self.c, self.s]
        self.copies = [
            send(axis, peer, mine, mine, self.sems, self.next_sem()) for peer in peers_of(axis)
        ]

    def start5(self):
        self.wait()
        axis = self.order[0]
        if axis == "rows":
            mine = self.pots.at[self.r, :, self.s]
        else:
            mine = self.pots.at[:, self.c, self.s]
        self.copies = [
            send(axis, peer, mine, mine, self.sems, self.next_sem()) for peer in peers_of(axis)
        ]

    def start6(self):
        self.wait()
        (peer,) = peers_of("slab")
        mine = self.pots.at[:, :, self.s]
        self.copies = [send("slab", peer, mine, mine, self.sems, self.next_sem())]


ORDERS = (("cols", "rows"), ("rows", "cols"))


def exchange_scratch(nr, nc, ns, own):
    kinds = []
    for order in ORDERS:
        first, second = (nr, nc) if order[0] == "rows" else (nc, nr)
        kinds += [
            pltpu.VMEM((nr, nc, own, TILE), jnp.bfloat16),
            pltpu.VMEM((nr, nc, own, TILE), jnp.bfloat16),
            pltpu.VMEM((first - 1, second, own, TILE), jnp.bfloat16),
            pltpu.VMEM((second, own, TILE), jnp.bfloat16),
            pltpu.VMEM((second - 1, own, TILE), jnp.bfloat16),
            pltpu.SemaphoreType.DMA((2, 2 * (nr + nc))),
        ]
    return kinds


def exchange_kernel(grid_ref, ext_ref, density_ref, pots_ref, *scratch):
    greet()
    parts = []
    for h, order in enumerate(ORDERS):
        bufs = scratch[6 * h : 6 * h + 6]
        parts.append(Exchange(order, grid_ref.at[h], pots_ref.at[h], bufs[:5], bufs[5]))
    for part in parts:
        part.start1()
    for part in parts:
        part.start2()
    for part in parts:
        part.start3()
    for h, part in enumerate(parts):
        density = part.finish()
        columns = pl.ds(h * TILE, TILE)
        density_ref[:, columns] = density
        part.start4(ext_ref[:, columns] + 0.5 * density)
    for part in parts:
        part.start5()
    for part in parts:
        part.start6()
    for part in parts:
        part.wait()


def local(
    density_blocks, block_owner, block_plane, block_segment, block_kinds, basis, ext_potential
):
    count = density_blocks.shape[0]
    kinds, width, cells = basis.shape
    zplanes = ext_potential.shape[0]
    segs = ext_potential.shape[1] // SEGW
    nz = zplanes * lax.axis_size(AXES)
    first = block_owner[:, 0] * zplanes + block_plane
    planes = (first[None, :] + jnp.arange(CZB, dtype=jnp.int32)[:, None]) % nz
    rowid = (planes * segs + block_segment[None, :]).reshape(-1)
    flat_basis = basis.reshape(kinds * width, cells)
    hot = block_kinds[:, 1][:, None] == jnp.arange(kinds, dtype=jnp.int32)[None, :]
    cubes = density_blocks.reshape(count, width, 1, width)
    wide = jnp.where(hot[:, None, :, None], cubes, jnp.zeros((), jnp.bfloat16))
    wide = wide.reshape(count * width, kinds * width)
    places = CZB * count

    grid = pl.pallas_call(
        functools.partial(deposit_kernel, width, count),
        out_shape=jax.ShapeDtypeStruct((SEGW // TILE, nz * segs, TILE), jnp.bfloat16),
        in_specs=[SMEM, VMEM, VMEM, VMEM],
        out_specs=VMEM,
        scratch_shapes=[pltpu.VMEM((places, SEGW), jnp.float32)],
        compiler_params=pltpu.CompilerParams(vmem_limit_bytes=50 << 20),
    )(block_kinds, rowid.reshape(1, places), wide, flat_basis)

    nr, nc, ns = (lax.axis_size(axis) for axis in AXES)
    own = zplanes * segs
    split_grid = (SEGW // TILE, nr, nc, ns, own, TILE)
    density, pots = pl.pallas_call(
        exchange_kernel,
        out_shape=(
            jax.ShapeDtypeStruct((own, SEGW), jnp.float32),
            jax.ShapeDtypeStruct(split_grid, jnp.bfloat16),
        ),
        in_specs=[VMEM, VMEM],
        out_specs=(VMEM, VMEM),
        scratch_shapes=exchange_scratch(nr, nc, ns, own),
        compiler_params=pltpu.CompilerParams(
            collective_id=0, has_side_effects=True, vmem_limit_bytes=50 << 20
        ),
    )(grid.reshape(split_grid), ext_potential.reshape(own, SEGW))
    pots = pots.reshape(SEGW // TILE, nz * segs, TILE)

    blocks = pl.pallas_call(
        functools.partial(integrate_kernel, width, count),
        out_shape=jax.ShapeDtypeStruct((count * width, width), jnp.bfloat16),
        in_specs=[SMEM, VMEM, VMEM, VMEM],
        out_specs=VMEM,
        scratch_shapes=[
            pltpu.VMEM((places, SEGW), jnp.float32),
            pltpu.VMEM((8 * width, cells), jnp.bfloat16),
        ],
        compiler_params=pltpu.CompilerParams(vmem_limit_bytes=50 << 20),
    )(block_kinds, rowid.reshape(places, 1), pots, flat_basis)
    return density.reshape(zplanes, -1), blocks.reshape(count, width * width)


def solution(mesh):
    split = P(AXES, None)
    return jax.shard_map(
        local,
        mesh=mesh,
        in_specs=(split, split, P(AXES), P(AXES), split, P(), split),
        out_specs=(split, split),
        check_vma=False,
    )
```

time: 642 us -> 98 us (0.15)
  matrix products: 482 us -> 0 us
  Pallas kernels: 0 us -> 76.3 us
  waiting for transfers between devices: 63.2 us -> 0 us
  local copies, waits for them, and re-layouts: 42.2 us -> 15.3 us
  loops' own time: 15.9 us -> 0 us
  starting transfers between devices: 15.9 us -> 0 us
  other arithmetic: 16.8 us -> 5.05 us
    dot_general x32 -> x0, matrix products: 482 us -> none  [the longest x4 201 us: deposit(): jnp.einsum('bmn,bnc->bmc', block_batch, col_basis, preferred_element_type...]
    pallas_call x0 -> x3, Pallas kernels: none -> 76.3 us  [the longest x1 42.5 us: local(): pl.pallas_call(exchange_kernel, out_shape=(jax.ShapeDtypeStruct((own, SEG...]
    all_to_all x3 -> x0, waiting for transfers between devices: 53.1 us -> none  [the longest x1 26.2 us: local(): lax.all_to_all(matrix_slots, ('rows', 'cols', 'slab'), split_axis=0, conc...]
    mul x12 -> x0, local copies, waits for them, and re-layouts: 21.5 us -> none  [the longest x8 21.1 us: placement(): place = plane_hot[:, :, :, None] * seg_hot[:, None, None, :]]
    another operation x2 -> x0, loops' own time: 15.9 us -> none  [the longest x1 15.7 us: local(): lax.scan(deposit, jnp.zeros((extended_rows, SEGW), jnp.float32), (block_b...]
    all_to_all x3 -> x0, starting transfers between devices: 15.7 us -> none  [the longest x1 7.3 us: local(): lax.all_to_all(send_meta, ('rows', 'cols', 'slab'), split_axis=0, concat_...]
    mul x8 -> x0, other arithmetic: 12.9 us -> none  [placement(): place = plane_hot[:, :, :, None] * seg_hot[:, None, None, :]]
    ppermute x2 -> x0, waiting for transfers between devices: 10.1 us -> none  [shifted(): return lax.ppermute(x, axis, [(i, (i + by) % size) for i in range(size)])]
  transfers between devices with their start and end apart: 5 -> 0, of which waited for: 5 -> 0; matrix products, arithmetic and copies ran while one was open for 1% -> 0% of each run, Pallas kernels for 0% -> 0%
where the time goes in v1:
time: 98 us; the launch traced here: 97.4 us
  Pallas kernels  76.3 us (78%)
  local copies, waits for them, and re-layouts  15.3 us (16%)
  other arithmetic  5.05 us (5%)
    pallas_call x1, Pallas kernels, local(): pl.pallas_call(exchange_kernel, out_shape=(jax.ShapeDtypeStruct((own, SEG...  42.5 us
    pallas_call x1, Pallas kernels, local(): pl.pallas_call(functools.partial(deposit_kernel, width, count), out_shape...  16.9 us
    pallas_call x1, Pallas kernels, local(): pl.pallas_call(functools.partial(integrate_kernel, width, count), out_sha...  16.9 us
    select_n x1, local copies, waits for them, and re-layouts, local(): wide = jnp.where(hot[:, None, :, None], cubes, jnp.zeros((), jnp.bfloat16))  6.96 us
    select_n x1, other arithmetic, local(): wide = jnp.where(hot[:, None, :, None], cubes, jnp.zeros((), jnp.bfloat16))  4.16 us
    reshape x2, local copies, waits for them, and re-layouts, local(): return (density.reshape(zplanes, -1), blocks.reshape(count, width * width))  2.3 us
    unnamed x5, local copies, waits for them, and re-layouts  2.1 us
    broadcast_in_dim x1, local copies, waits for them, and re-layouts, local(): wide = jnp.where(hot[:, None, :, None], cubes, jnp.zeros((), jnp.bfloat16))  2.05 us

profile of v1, /device:TPU:0, one launch (start us, length us, event | category | flops | bytes accessed | tf_op | source)
XLA Modules:
  0.0 97.4 jit_solution(17768173029171147451)
XLA Ops:
  0.6 0.7 bitcast_add_fusion
  1.3 0.1 add.90
  1.4 0.7 add.92
  2.0 0.1 add.93
  2.1 0.8 copy.17.kinds_ref
  2.9 2.1 %broadcast_in_dim.28 = bf16[64,64,64]{2,1,0:T(8,128)(2,1)S(1)} reshape(bf16[64,4096]{1,0:T(8,128)(2,1)} %param.7) | data formatting | bytes 1048576 | tf_op jit(solution)/shard_map/jit(_where)/broadcast_in_dim | solution.py:296
  5.0 0.7 slice_bitcast_fusion
  5.7 0.1 iota_compare_fusion
  5.7 4.2 %broadcast_select_fusion = bf16[64,64,4,64]{3,2,1,0:T(4,128)(2,1)} fusion(pred[64,4]{1,0:T(8,128)(4,1)S(1)} %iota_compare_fusion, bf16[64,64,64]{2,1,0:T(8,128)(2,1)S(1)} %broadcast_in_dim.28), kind=kLoop, calls=%fused_computation | loop fusion | flops 1048576 | bytes 2621696 | tf_op jit(solution)/shard_map/jit(_where)/select_n | solution.py:296
  9.9 7.0 %select_n.33.wide_ref = bf16[4096,256]{1,0:T(8,128)(2,1)} reshape(bf16[64,64,4,64]{3,2,1,0:T(4,128)(2,1)} %broadcast_select_fusion) | data formatting | bytes 4194304 | tf_op jit(solution)/shard_map/jit(_where)/select_n | solution.py:296
  16.9 0.0 copy-start.1
  16.9 16.9 %shard_map.86 = bf16[2,2048,256]{2,1,0:T(8,128)(2,1)S(1)} custom-call(s32[64,2]{1,0:T(8,128)S(1)} %copy.17.kinds_ref, s32[1,512]{1,0:T(1,128)S(1)} %fusion.4.rows_ref, bf16[4096,256]{1,0:T(8,128)(2,1)} %select_n.33.wide_ref, bf16[256,4096]{1,0:T(8,128)(2,1)} %bitcast.9), custom_call_target="tpu_custom_call" | custom-call | tf_op jit(solution)/shard_map/pallas_call | solution.py:300
  33.8 0.0 copy-start
  33.8 1.3 %copy-done = bf16[2,2048,256]{2,1,0:T(8,128)(2,1)} copy-done((bf16[2,2048,256]{2,1,0:T(8,128)(2,1)}, bf16[2,2048,256]{2,1,0:T(8,128)(2,1)S(1)}, u32[]{:S(2)}) %copy-start) | copy-done | bytes 2097176
  35.1 0.0 copy-done.1
  35.2 42.5 %shard_map.87 = (f32[64,512]{1,0:T(8,128)S(1)}, bf16[2,4,4,2,64,256]{5,4,3,2,1,0:T(8,128)(2,1)S(1)}) custom-call(bf16[2,4,4,2,64,256]{5,4,3,2,1,0:T(8,128)(2,1)} %bitcast.7, f32[64,512]{1,0:T(8,128)S(1)} %reshape.196.ext_ref), custom_call_target="tpu_custom_call" | custom-call | tf_op jit(solution)/shard_map/pallas_call | solution.py:312
  77.7 0.2 add.99
  77.9 0.2 add.100
  78.1 0.1 fusion.2.rows_ref
  78.2 16.9 %shard_map.88 = bf16[4096,64]{1,0:T(8,128)(2,1)S(1)} custom-call(s32[64,2]{1,0:T(8,128)S(1)} %copy.17.kinds_ref, s32[512,1]{1,0:T(8,128)S(1)} %fusion.2.rows_ref, bf16[2,2048,256]{2,1,0:T(8,128)(2,1)S(1)} %bitcast.8, bf16[256,4096]{1,0:T(8,128)(2,1)} %bitcast.10), custom_call_target="tpu_custom_call" | custom-call | tf_op jit(solution)/shard_map/pallas_call | solution.py:327
  95.1 1.6 %reshape.199 = bf16[64,4096]{1,0:T(8,128)(2,1)} reshape(bf16[4096,64]{1,0:T(8,128)(2,1)S(1)} %shard_map.88) | data formatting | bytes 1048576 | tf_op jit(solution)/shard_map/reshape | solution.py:338
  96.7 0.7 reshape.197
  (3 shorter events, 0.0 us)
Async XLA Ops:
  16.9 18.3 %copy-start.1 = (f32[8,4096]{1,0:T(8,128)S(1)}, f32[8,4096]{1,0:T(8,128)}, u32[]{:S(2)}) copy-start(f32[8,4096]{1,0:T(8,128)} %param.13) | copy-start | bytes 393220
  33.8 1.3 %copy-start = (bf16[2,2048,256]{2,1,0:T(8,128)(2,1)}, bf16[2,2048,256]{2,1,0:T(8,128)(2,1)S(1)}, u32[]{:S(2)}) copy-start(bf16[2,2048,256]{2,1,0:T(8,128)(2,1)S(1)} %shard_map.86) | copy-start | bytes 6291460

commit v2 on v1

v2 whole, which is shorter than its diff:
```python
import functools

import jax
import jax.numpy as jnp
from jax import lax
from jax.experimental import pallas as pl
from jax.experimental.pallas import tpu as pltpu
from jax.sharding import PartitionSpec as P

CZB = 8
SEGW = 512
TILE = 256
AXES = ("rows", "cols", "slab")
VMEM = pl.BlockSpec(memory_space=pltpu.VMEM)
MESH = pl.DeviceIdType.MESH
SMEM = pl.BlockSpec(memory_space=pltpu.SMEM)


def peers_of(axis):
    size = lax.axis_size(axis)
    me = lax.axis_index(axis)
    return [lax.rem(me + o, size) for o in range(1, size)]


def greet():
    barrier = pltpu.get_barrier_semaphore()
    total = 0
    for axis in AXES:
        for peer in peers_of(axis):
            pl.semaphore_signal(barrier, inc=1, device_id={axis: peer}, device_id_type=MESH)
            total += 1
    pl.semaphore_wait(barrier, total)


def send(axis, peer, src, dst, sems, at):
    copy = pltpu.make_async_remote_copy(
        src_ref=src,
        dst_ref=dst,
        send_sem=sems.at[0, at],
        recv_sem=sems.at[1, at],
        device_id={axis: peer},
        device_id_type=MESH,
    )
    copy.start()
    return copy


class Exchange:
    def __init__(self, order, grid, pots, bufs, sems):
        self.order, self.grid, self.pots, self.sems = order, grid, pots, sems
        self.got1, self.sum1, self.got2, self.sum2, self.got3 = bufs
        self.r, self.c, self.s = (lax.axis_index(axis) for axis in AXES)
        self.sizes = {axis: lax.axis_size(axis) for axis in AXES}
        self.used = 0

    def next_sem(self):
        self.used += 1
        return self.used - 1

    def start1(self):
        (peer,) = peers_of("slab")
        self.copies = [
            send("slab", peer, self.grid.at[:, :, peer], self.got1, self.sems, self.next_sem())
        ]

    def wait(self):
        for copy in self.copies:
            copy.wait()

    def start2(self):
        self.wait()
        nr, nc = self.sizes["rows"], self.sizes["cols"]

        def add(n, carry):
            r, c = n // nc, n % nc
            self.sum1[r, c] = (
                self.grid[r, c, self.s].astype(jnp.float32) + self.got1[r, c].astype(jnp.float32)
            ).astype(jnp.bfloat16)
            return carry

        lax.fori_loop(0, nr * nc, add, 0)
        axis = self.order[0]
        self.copies = []
        for o, peer in enumerate(peers_of(axis)):
            src = self.sum1.at[peer] if axis == "rows" else self.sum1.at[:, peer]
            self.copies.append(send(axis, peer, src, self.got2.at[o], self.sems, self.next_sem()))

    def start3(self):
        self.wait()
        first, axis = self.order

        def add(n, carry):
            mine = self.sum1[self.r, n] if first == "rows" else self.sum1[n, self.c]
            total = mine.astype(jnp.float32)
            for o in range(self.sizes[first] - 1):
                total = total + self.got2[o, n].astype(jnp.float32)
            self.sum2[n] = total.astype(jnp.bfloat16)
            return carry

        lax.fori_loop(0, self.sizes[axis], add, 0)
        self.copies = []
        for o, peer in enumerate(peers_of(axis)):
            self.copies.append(
                send(axis, peer, self.sum2.at[peer], self.got3.at[o], self.sems, self.next_sem())
            )

    def finish(self):
        self.wait()
        axis = self.order[1]
        total = self.sum2[self.r if axis == "rows" else self.c].astype(jnp.float32)
        for o in range(self.sizes[axis] - 1):
            total = total + self.got3[o].astype(jnp.float32)
        return total

    def start4(self, potential):
        self.pots[self.r, self.c, self.s] = potential.astype(jnp.bfloat16)
        axis = self.order[1]
        mine = self.pots.at[self.r, self.c, self.s]
        self.copies = [
            send(axis, peer, mine, mine, self.sems, self.next_sem()) for peer in peers_of(axis)
        ]

    def start5(self):
        self.wait()
        axis = self.order[0]
        if axis == "rows":
            mine = self.pots.at[self.r, :, self.s]
        else:
            mine = self.pots.at[:, self.c, self.s]
        self.copies = [
            send(axis, peer, mine, mine, self.sems, self.next_sem()) for peer in peers_of(axis)
        ]

    def start6(self):
        self.wait()
        (peer,) = peers_of("slab")
        mine = self.pots.at[:, :, self.s]
        self.copies = [send("slab", peer, mine, mine, self.sems, self.next_sem())]


ORDERS = (("cols", "rows"), ("rows", "cols"))


def exchange_scratch(nr, nc, ns, own):
    kinds = []
    for order in ORDERS:
        first, second = (nr, nc) if order[0] == "rows" else (nc, nr)
        kinds += [
            pltpu.VMEM((nr, nc, own, TILE), jnp.bfloat16),
            pltpu.VMEM((nr, nc, own, TILE), jnp.bfloat16),
            pltpu.VMEM((first - 1, second, own, TILE), jnp.bfloat16),
            pltpu.VMEM((second, own, TILE), jnp.bfloat16),
            pltpu.VMEM((second - 1, own, TILE), jnp.bfloat16),
            pltpu.SemaphoreType.DMA((2, 2 * (nr + nc))),
        ]
    return kinds


def fused_kernel(
    width,
    count,
    kinds_ref,
    row_ref,
    column_ref,
    blocks_ref,
    basis_ref,
    ext_ref,
    density_ref,
    out_ref,
    halves_ref,
    wide_ref,
    tiles_ref,
    grid_ref,
    pots_ref,
    weighted_ref,
    full_ref,
    *scratch,
):
    group = 8
    groups = count // group
    kinds = basis_ref.shape[0]
    nr, nc, ns, own = grid_ref.shape[1:5]
    places = tiles_ref.shape[0]

    for h in range(SEGW // TILE):
        for i in range(CZB):
            halves_ref[h, :, :, i * TILE : (i + 1) * TILE] = basis_ref[
                :, :, i * SEGW + h * TILE : i * SEGW + (h + 1) * TILE
            ]

    lane_kind = lax.broadcasted_iota(jnp.int32, (width, kinds * width), 1) // width
    for k in range(count):
        lines = blocks_ref[k * width : (k + 1) * width, :]
        copies = jnp.concatenate([lines] * kinds, axis=1)
        wide_ref[k * width : (k + 1) * width, :] = jnp.where(
            lane_kind == kinds_ref[k, 1], copies, jnp.zeros_like(copies)
        )

    def of_kind(h, kind, columns):
        return halves_ref[h, kind, :, columns]

    def deposit(h, first, last):
        def column_tile(i, carry):
            columns = pl.ds(pl.multiple_of(i * TILE, TILE), TILE)
            weights = halves_ref[h, :, :, columns].reshape(kinds * width, TILE)
            for g in range(groups):
                lhs = wide_ref[g * group * width : (g + 1) * group * width, :]
                half = jnp.dot(lhs, weights, preferred_element_type=jnp.float32)
                sums = []
                for b in range(group):
                    a = of_kind(h, kinds_ref[g * group + b, 0], columns)
                    product = a.astype(jnp.float32) * half[b * width : (b + 1) * width]
                    sums.append(jnp.sum(product, axis=0, keepdims=True))
                row = pl.multiple_of(i * count + g * group, group)
                tiles_ref[pl.ds(row, group), :] = jnp.concatenate(sums, axis=0)
            return carry

        lax.fori_loop(first, last, column_tile, 0)

    def place(h):
        tiles = tiles_ref[...].astype(jnp.bfloat16)

        def one(n, carry):
            r, c = n // nc, n % nc
            rows = lax.broadcasted_iota(jnp.int32, (ns * own, places), 0) + n * ns * own
            hot = jnp.where(row_ref[...] == rows, 1.0, 0.0).astype(jnp.bfloat16)
            placed = jnp.dot(hot, tiles, preferred_element_type=jnp.float32).astype(jnp.bfloat16)
            for s in range(ns):
                grid_ref[h, r, c, s] = placed[s * own : (s + 1) * own]
            return carry

        lax.fori_loop(0, nr * nc, one, 0)

    def gather(h):
        tiles_ref[...] = jnp.zeros_like(tiles_ref)

        def one(r, carry):
            rows = nc * ns * own
            values = pots_ref[h, r].reshape(rows, TILE)
            places_of = lax.broadcasted_iota(jnp.int32, (places, rows), 1) + r * rows
            hot = jnp.where(column_ref[...] == places_of, 1.0, 0.0).astype(jnp.bfloat16)
            tiles_ref[...] += jnp.dot(hot, values, preferred_element_type=jnp.float32)
            return carry

        lax.fori_loop(0, nr, one, 0)

    def integrate(h, first, last):
        def block_group(g, carry):
            for i in range(CZB):
                rows = pl.ds(pl.multiple_of(i * count + g * group, group), group)
                pots = tiles_ref[rows, :]
                columns = pl.ds(i * TILE, TILE)
                for b in range(group):
                    a = of_kind(h, kinds_ref[g * group + b, 0], columns)
                    row = jnp.broadcast_to(pots[b : b + 1], (width, TILE)).astype(jnp.bfloat16)
                    weighted_ref[b * width : (b + 1) * width, i * TILE : (i + 1) * TILE] = a * row
            full = lax.dot_general(
                weighted_ref[...],
                halves_ref[h].reshape(kinds * width, CZB * TILE),
                (((1,), (1,)), ((), ())),
                preferred_element_type=jnp.float32,
            )
            lines = pl.ds(pl.multiple_of(g * group * width, group * width), group * width)
            if h < SEGW // TILE - 1:
                if h > 0:
                    full = full + full_ref[lines, :]
                full_ref[lines, :] = full
                return carry
            full = full + full_ref[lines, :]
            for b in range(group):
                kind = kinds_ref[g * group + b, 1]
                mine = jnp.where(lane_kind == kind, full[b * width : (b + 1) * width], 0.0)
                picked = mine[:, :width]
                for k in range(1, kinds):
                    picked = picked + mine[:, k * width : (k + 1) * width]
                out_ref[pl.ds(pl.multiple_of((g * group + b) * width, width), width), :] = (
                    picked.astype(jnp.bfloat16)
                )
            return carry

        lax.fori_loop(first, last, block_group, 0)

    parts = []
    for h, order in enumerate(ORDERS):
        bufs = scratch[6 * h : 6 * h + 6]
        parts.append(Exchange(order, grid_ref.at[h], pots_ref.at[h], bufs[:5], bufs[5]))
    early, late = parts

    def settle(h):
        density = parts[h].finish()
        columns = pl.ds(h * TILE, TILE)
        density_ref[:, columns] = density
        parts[h].start4(ext_ref[:, columns] + 0.5 * density)

    deposit(0, 0, CZB)
    place(0)
    greet()
    early.start1()
    deposit(1, 0, 2)
    early.start2()
    deposit(1, 2, 6)
    early.start3()
    deposit(1, 6, CZB)
    place(1)
    late.start1()
    settle(0)
    late.start2()
    early.start5()
    late.start3()
    early.start6()
    settle(1)
    early.wait()
    gather(0)
    integrate(0, 0, groups // 2)
    late.start5()
    integrate(0, groups // 2, groups)
    late.start6()
    late.wait()
    gather(1)
    integrate(1, 0, groups)


def local(
    density_blocks, block_owner, block_plane, block_segment, block_kinds, basis, ext_potential
):
    count = density_blocks.shape[0]
    kinds, width, cells = basis.shape
    zplanes = ext_potential.shape[0]
    segs = ext_potential.shape[1] // SEGW
    nz = zplanes * lax.axis_size(AXES)
    first = block_owner[:, 0] * zplanes + block_plane
    planes = (first[None, :] + jnp.arange(CZB, dtype=jnp.int32)[:, None]) % nz
    rowid = (planes * segs + block_segment[None, :]).reshape(-1)
    places = CZB * count

    nr, nc, ns = (lax.axis_size(axis) for axis in AXES)
    own = zplanes * segs
    halves = SEGW // TILE
    density, blocks = pl.pallas_call(
        functools.partial(fused_kernel, width, count),
        out_shape=(
            jax.ShapeDtypeStruct((own, SEGW), jnp.float32),
            jax.ShapeDtypeStruct((count * width, width), jnp.bfloat16),
        ),
        in_specs=[SMEM, VMEM, VMEM, VMEM, VMEM, VMEM],
        out_specs=(VMEM, VMEM),
        scratch_shapes=[
            pltpu.VMEM((halves, kinds, width, cells // halves), jnp.bfloat16),
            pltpu.VMEM((count * width, kinds * width), jnp.bfloat16),
            pltpu.VMEM((places, TILE), jnp.float32),
            pltpu.VMEM((halves, nr, nc, ns, own, TILE), jnp.bfloat16),
            pltpu.VMEM((halves, nr, nc, ns, own, TILE), jnp.bfloat16),
            pltpu.VMEM((8 * width, cells // halves), jnp.bfloat16),
            pltpu.VMEM((count * width, kinds * width), jnp.float32),
            *exchange_scratch(nr, nc, ns, own),
        ],
        compiler_params=pltpu.CompilerParams(
            collective_id=0, has_side_effects=True, vmem_limit_bytes=60 << 20
        ),
    )(
        block_kinds,
        rowid.reshape(1, places),
        rowid.reshape(places, 1),
        density_blocks.reshape(count * width, width),
        basis,
        ext_potential.reshape(own, SEGW),
    )
    return density.reshape(zplanes, -1), blocks.reshape(count, width * width)


def solution(mesh):
    split = P(AXES, None)
    return jax.shard_map(
        local,
        mesh=mesh,
        in_specs=(split, split, P(AXES), P(AXES), split, P(), split),
        out_specs=(split, split),
        check_vma=False,
    )
```

time: 98 us -> 90.8 us (0.927)
  local copies, waits for them, and re-layouts: 15.3 us -> 11.2 us
  other arithmetic: 5.05 us -> 2.1 us
    select_n x1 -> x0, local copies, waits for them, and re-layouts: 6.96 us -> none  [local(): wide = jnp.where(hot[:, None, :, None], cubes, jnp.zeros((), jnp.bfloat16))]
    select_n x1 -> x0, other arithmetic: 4.16 us -> none  [local(): wide = jnp.where(hot[:, None, :, None], cubes, jnp.zeros((), jnp.bfloat16))]
    reshape x0 -> x1, local copies, waits for them, and re-layouts: none -> 2.75 us  [local(): density_blocks.reshape(count * width, width)]
    broadcast_in_dim x1 -> x0, local copies, waits for them, and re-layouts: 2.05 us -> none  [local(): wide = jnp.where(hot[:, None, :, None], cubes, jnp.zeros((), jnp.bfloat16))]
    reshape x2, local copies, waits for them, and re-layouts: 2.3 us -> 4.3 us  [local(): return (density.reshape(zplanes, -1), blocks.reshape(count, width * width))]
    reshape x1, local copies, waits for them, and re-layouts: 0.03 us -> 1.59 us  [local(): ext_potential.reshape(own, SEGW)]
    add x2, other arithmetic: 0.13 us -> 1.42 us  [local(): rowid = (planes * segs + block_segment[None, :]).reshape(-1)]
    unnamed x5 -> x1, local copies, waits for them, and re-layouts: 2.1 us -> 1.38 us
where the time goes in v2:
time: 90.8 us; the launch traced here: 90.6 us
  Pallas kernels  76.6 us (84%)
  local copies, waits for them, and re-layouts  11.2 us (12%)
  other arithmetic  2.1 us (2%)
    pallas_call x1, Pallas kernels, local(): pl.pallas_call(functools.partial(fused_kernel, width, count), out_shape=(...  76.6 us
    reshape x2, local copies, waits for them, and re-layouts, local(): return (density.reshape(zplanes, -1), blocks.reshape(count, width * width))  4.3 us
    reshape x1, local copies, waits for them, and re-layouts, local(): density_blocks.reshape(count * width, width)  2.75 us

profile of v2, /device:TPU:0, one launch (start us, length us, event | category | flops | bytes accessed | tf_op | source)
XLA Modules:
  0.0 90.6 jit_solution(6053923740813397378)
XLA Ops:
  0.6 0.7 bitcast_add_fusion
  1.3 0.1 add.90
  1.4 0.7 add.92
  2.0 0.1 add.93
  2.1 0.6 fusion.4.row_ref
  2.7 1.4 %copy.20.kinds_ref = s32[64,2]{1,0:T(8,128)} copy(s32[64,2]{0,1:T(2,128)} %param.11) | data formatting | bytes 1024 | tf_op args[4]
  4.1 1.6 %reshape.161.ext_ref = f32[64,512]{1,0:T(8,128)} reshape(f32[8,4096]{1,0:T(8,128)} %param.13) | data formatting | bytes 262144 | tf_op jit(solution)/shard_map/reshape | solution.py:366
  5.7 0.2 add.100
  5.9 0.2 add.99
  6.1 0.8 fusion.2.column_ref
  6.9 2.8 %reshape.160.blocks_ref = bf16[4096,64]{1,0:T(8,128)(2,1)} reshape(bf16[64,4096]{1,0:T(8,128)(2,1)} %param.7) | data formatting | bytes 1048576 | tf_op jit(solution)/shard_map/reshape | solution.py:364
  9.7 76.6 %shard_map.86 = (f32[64,512]{1,0:T(8,128)}, bf16[4096,64]{1,0:T(8,128)(2,1)}) custom-call(s32[64,2]{1,0:T(8,128)} %copy.20.kinds_ref, s32[1,512]{1,0:T(1,128)} %fusion.4.row_ref, s32[512,1]{1,0:T(8,128)} %fusion.2.column_ref, bf16[4096,64]{1,0:T(8,128)(2,1)} %reshape.160.blocks_ref, bf16[4,64,4096]{2,1,0:T(8,128)(2,1)} %basis_ref.1, f32[64,512]{1,0:T(8,128)} %reshape.161.ext_ref), custom_call_target="tpu_custom_call" | custom-call | tf_op jit(solution)/shard_map/pallas_call | solution.py:339
  86.3 1.6 %reshape.162 = f32[8,4096]{1,0:T(8,128)} reshape(f32[64,512]{1,0:T(8,128)} %get-tuple-element.4) | data formatting | bytes 262144 | tf_op jit(solution)/shard_map/reshape | solution.py:368
  87.9 2.7 %reshape.163 = bf16[64,4096]{1,0:T(8,128)(2,1)} reshape(bf16[4096,64]{1,0:T(8,128)(2,1)} %get-tuple-element.5) | data formatting | bytes 1048576 | tf_op jit(solution)/shard_map/reshape | solution.py:368
  (1 shorter events, 0.0 us)

commit v3 on v2

v3 whole, which is shorter than its diff:
```python
import functools

import jax
import jax.numpy as jnp
from jax import lax
from jax.experimental import pallas as pl
from jax.experimental.pallas import tpu as pltpu
from jax.sharding import PartitionSpec as P

CZB = 8
SEGW = 512
TILE = 256
AXES = ("rows", "cols", "slab")
VMEM = pl.BlockSpec(memory_space=pltpu.VMEM)
MESH = pl.DeviceIdType.MESH
SMEM = pl.BlockSpec(memory_space=pltpu.SMEM)


def peers_of(axis):
    size = lax.axis_size(axis)
    me = lax.axis_index(axis)
    return [lax.rem(me + o, size) for o in range(1, size)]


def greet():
    barrier = pltpu.get_barrier_semaphore()
    total = 0
    for axis in AXES:
        for peer in peers_of(axis):
            pl.semaphore_signal(barrier, inc=1, device_id={axis: peer}, device_id_type=MESH)
            total += 1
    pl.semaphore_wait(barrier, total)


class Exchange:
    def __init__(self, grid, pots, bufs):
        self.grid, self.pots = grid, pots
        self.got1, self.sum1, self.got2, self.sum2, self.got3, self.sems = bufs
        self.r, self.c, self.s = (lax.axis_index(axis) for axis in AXES)
        self.nr, self.nc = (lax.axis_size(axis) for axis in AXES[:2])
        (self.twin,) = peers_of("slab")
        self.used = 0

    def send(self, axis, peer, src, dst):
        copy = pltpu.make_async_remote_copy(
            src_ref=src,
            dst_ref=dst,
            send_sem=self.sems.at[0, self.used],
            recv_sem=self.sems.at[1, self.used],
            device_id={axis: peer},
            device_id_type=MESH,
        )
        copy.start()
        self.used += 1
        return copy

    def toward(self, piece):
        return lax.rem(self.r + 1 + piece, self.nr)

    def reduce_slab(self):
        self.slab = [
            self.send("slab", self.twin, self.grid.at[self.toward(p), :, self.twin], self.got1.at[p])
            for p in range(self.nr)
        ]
        self.cols, self.rows = [], []

    def reduce_cols(self, p):
        self.slab[p].wait()
        row = self.toward(p)
        for c in range(self.nc):
            self.sum1[p, c] = (
                self.grid[row, c, self.s].astype(jnp.float32) + self.got1[p, c].astype(jnp.float32)
            ).astype(jnp.bfloat16)
        self.cols.append(
            [
                self.send("cols", peer, self.sum1.at[p, peer], self.got2.at[p, o])
                for o, peer in enumerate(peers_of("cols"))
            ]
        )

    def reduce_rows(self, p):
        for copy in self.cols[p]:
            copy.wait()
        total = self.sum1[p, self.c].astype(jnp.float32)
        for o in range(self.nc - 1):
            total = total + self.got2[p, o].astype(jnp.float32)
        self.sum2[p] = total.astype(jnp.bfloat16)
        if p < self.nr - 1:
            self.rows.append(
                self.send("rows", self.toward(p), self.sum2.at[p], self.got3.at[p])
            )

    def finish(self):
        for copy in self.rows:
            copy.wait()
        total = self.sum2[self.nr - 1].astype(jnp.float32)
        for p in range(self.nr - 1):
            total = total + self.got3[p].astype(jnp.float32)
        return total

    def spread_cols(self, row):
        mine = self.pots.at[row, self.c, self.s]
        self.cols.append([self.send("cols", peer, mine, mine) for peer in peers_of("cols")])

    def spread_rows(self, potential):
        self.pots[self.r, self.c, self.s] = potential.astype(jnp.bfloat16)
        mine = self.pots.at[self.r, self.c, self.s]
        self.rows = [
            self.send("rows", self.toward(p), mine, mine) for p in range(self.nr - 1)
        ]
        self.cols = []
        self.spread_cols(self.r)

    def source(self, piece):
        return lax.rem(self.r + self.nr - piece, self.nr)

    def pass_cols(self):
        for p in range(self.nr - 1):
            self.rows[p].wait()
            self.spread_cols(self.source(p + 1))

    def pass_slab(self):
        self.slab = []
        for p in range(self.nr):
            for copy in self.cols[p]:
                copy.wait()
            mine = self.pots.at[self.source(p), :, self.s]
            self.slab.append(self.send("slab", self.twin, mine, mine))

    def wait(self):
        for copy in self.slab:
            copy.wait()


def exchange_scratch(nr, nc, own):
    return [
        pltpu.VMEM((nr, nc, own, TILE), jnp.bfloat16),
        pltpu.VMEM((nr, nc, own, TILE), jnp.bfloat16),
        pltpu.VMEM((nr, nc - 1, own, TILE), jnp.bfloat16),
        pltpu.VMEM((nr, own, TILE), jnp.bfloat16),
        pltpu.VMEM((nr - 1, own, TILE), jnp.bfloat16),
        pltpu.SemaphoreType.DMA((2, 2 * (nr + nr * (nc - 1) + nr - 1))),
    ] * (SEGW // TILE)


def fused_kernel(
    width,
    count,
    codes_ref,
    blocks_ref,
    basis_ref,
    ext_ref,
    density_ref,
    out_ref,
    column_ref,
    halves_ref,
    wide_ref,
    tiles_ref,
    grid_ref,
    pots_ref,
    weighted_ref,
    full_ref,
    *scratch,
):
    group = 8
    groups = count // group
    kinds = basis_ref.shape[0]
    nr, nc, ns, own = grid_ref.shape[1:5]
    places = tiles_ref.shape[0]

    for h in range(SEGW // TILE):
        for i in range(CZB):
            halves_ref[h, :, :, i * TILE : (i + 1) * TILE] = basis_ref[
                :, :, i * SEGW + h * TILE : i * SEGW + (h + 1) * TILE
            ]

    total_rows = nr * nc * ns * own
    segs = own // density_ref.shape[0]
    block_of = lax.broadcasted_iota(jnp.int32, (count, 128), 0)
    lane_block = lax.broadcasted_iota(jnp.int32, (1, places), 1) % count
    base_column = jnp.zeros((count, 128), jnp.int32)
    base_row = jnp.zeros((1, places), jnp.int32)
    for k in range(count):
        base = lax.div(codes_ref[k], kinds * kinds)
        base_column = jnp.where(block_of == k, base, base_column)
        base_row = jnp.where(lane_block == k, base, base_row)
    for i in range(CZB):
        moved = base_column + i * segs
        column_ref[i * count : (i + 1) * count, :] = jnp.where(
            moved >= total_rows, moved - total_rows, moved
        )
    moved = base_row + lax.broadcasted_iota(jnp.int32, (1, places), 1) // count * segs
    row_of = jnp.where(moved >= total_rows, moved - total_rows, moved)

    lane_kind = lax.broadcasted_iota(jnp.int32, (width, kinds * width), 1) // width
    for k in range(count):
        lines = blocks_ref[k * width : (k + 1) * width, :]
        copies = jnp.concatenate([lines] * kinds, axis=1)
        wide_ref[k * width : (k + 1) * width, :] = jnp.where(
            lane_kind == lax.rem(codes_ref[k], kinds), copies, jnp.zeros_like(copies)
        )

    def of_kind(h, kind, columns):
        return halves_ref[h, kind, :, columns]

    def deposit(h, first, last):
        def column_tile(i, carry):
            columns = pl.ds(pl.multiple_of(i * TILE, TILE), TILE)
            weights = halves_ref[h, :, :, columns].reshape(kinds * width, TILE)
            for g in range(groups):
                lhs = wide_ref[g * group * width : (g + 1) * group * width, :]
                half = jnp.dot(lhs, weights, preferred_element_type=jnp.float32)
                sums = []
                for b in range(group):
                    a = of_kind(h, lax.rem(lax.div(codes_ref[g * group + b], kinds), kinds), columns)
                    product = a.astype(jnp.float32) * half[b * width : (b + 1) * width]
                    sums.append(jnp.sum(product, axis=0, keepdims=True))
                row = pl.multiple_of(i * count + g * group, group)
                tiles_ref[pl.ds(row, group), :] = jnp.concatenate(sums, axis=0)
            return carry

        if last > first:
            lax.fori_loop(first, last, column_tile, 0)

    def place(h):
        tiles = tiles_ref[...].astype(jnp.bfloat16)

        def one(n, carry):
            r, c = n // nc, n % nc
            rows = lax.broadcasted_iota(jnp.int32, (ns * own, places), 0) + n * ns * own
            hot = jnp.where(row_of == rows, 1.0, 0.0).astype(jnp.bfloat16)
            placed = jnp.dot(hot, tiles, preferred_element_type=jnp.float32).astype(jnp.bfloat16)
            for s in range(ns):
                grid_ref[h, r, c, s] = placed[s * own : (s + 1) * own]
            return carry

        lax.fori_loop(0, nr * nc, one, 0)

    def gather(h):
        tiles_ref[...] = jnp.zeros_like(tiles_ref)

        def one(r, carry):
            rows = nc * ns * own
            values = pots_ref[h, r].reshape(rows, TILE)
            column = jnp.concatenate([column_ref[...]] * (rows // 128), axis=1)
            places_of = lax.broadcasted_iota(jnp.int32, (places, rows), 1) + r * rows
            hot = jnp.where(column == places_of, 1.0, 0.0).astype(jnp.bfloat16)
            tiles_ref[...] += jnp.dot(hot, values, preferred_element_type=jnp.float32)
            return carry

        lax.fori_loop(0, nr, one, 0)

    def integrate(h, first, last):
        def block_group(g, carry):
            for i in range(CZB):
                rows = pl.ds(pl.multiple_of(i * count + g * group, group), group)
                pots = tiles_ref[rows, :]
                columns = pl.ds(i * TILE, TILE)
                for b in range(group):
                    a = of_kind(h, lax.rem(lax.div(codes_ref[g * group + b], kinds), kinds), columns)
                    row = jnp.broadcast_to(pots[b : b + 1], (width, TILE)).astype(jnp.bfloat16)
                    weighted_ref[b * width : (b + 1) * width, i * TILE : (i + 1) * TILE] = a * row
            full = lax.dot_general(
                weighted_ref[...],
                halves_ref[h].reshape(kinds * width, CZB * TILE),
                (((1,), (1,)), ((), ())),
                preferred_element_type=jnp.float32,
            )
            lines = pl.ds(pl.multiple_of(g * group * width, group * width), group * width)
            if h < SEGW // TILE - 1:
                if h > 0:
                    full = full + full_ref[lines, :]
                full_ref[lines, :] = full
                return carry
            full = full + full_ref[lines, :]
            for b in range(group):
                kind = lax.rem(codes_ref[g * group + b], kinds)
                mine = jnp.where(lane_kind == kind, full[b * width : (b + 1) * width], 0.0)
                picked = mine[:, :width]
                for k in range(1, kinds):
                    picked = picked + mine[:, k * width : (k + 1) * width]
                out_ref[pl.ds(pl.multiple_of((g * group + b) * width, width), width), :] = (
                    picked.astype(jnp.bfloat16)
                )
            return carry

        lax.fori_loop(first, last, block_group, 0)

    parts = []
    for h in range(SEGW // TILE):
        bufs = scratch[6 * h : 6 * h + 6]
        parts.append(Exchange(grid_ref.at[h], pots_ref.at[h], bufs))
    early, late = parts

    def settle(h):
        density = parts[h].finish().reshape(own // segs, segs, TILE)
        potential = []
        for s in range(segs):
            columns = pl.ds(s * SEGW + h * TILE, TILE)
            density_ref[:, columns] = density[:, s]
            potential.append(ext_ref[:, columns] + 0.5 * density[:, s])
        parts[h].spread_rows(jnp.stack(potential, axis=1).reshape(own, TILE))

    deposit(0, 0, CZB)
    place(0)
    greet()
    early.reduce_slab()
    deposit(1, 0, 1)
    for p in range(nr):
        early.reduce_cols(p)
    deposit(1, 1, 3)
    done = 3
    for p in range(nr):
        early.reduce_rows(p)
        more = 3 + (p + 1) * (CZB - 3) // nr
        deposit(1, done, more)
        done = more
    place(1)
    late.reduce_slab()
    settle(0)
    for p in range(nr):
        late.reduce_cols(p)
    early.pass_cols()
    for p in range(nr):
        late.reduce_rows(p)
    early.pass_slab()
    settle(1)
    early.wait()
    gather(0)
    integrate(0, 0, groups // 4)
    late.pass_cols()
    integrate(0, groups // 4, 5 * groups // 8)
    late.pass_slab()
    integrate(0, 5 * groups // 8, groups)
    late.wait()
    gather(1)
    integrate(1, 0, groups)


def local(
    density_blocks, block_owner, block_plane, block_segment, block_kinds, basis, ext_potential
):
    count = density_blocks.shape[0]
    kinds, width, cells = basis.shape
    zplanes = ext_potential.shape[0]
    segs = ext_potential.shape[1] // SEGW
    first = (block_owner[:, 0] * zplanes + block_plane) * segs + block_segment
    codes = (first * kinds + block_kinds[:, 0]) * kinds + block_kinds[:, 1]
    places = CZB * count

    nr, nc, ns = (lax.axis_size(axis) for axis in AXES)
    own = zplanes * segs
    halves = SEGW // TILE
    density, blocks = pl.pallas_call(
        functools.partial(fused_kernel, width, count),
        out_shape=(
            jax.ShapeDtypeStruct(ext_potential.shape, jnp.float32),
            jax.ShapeDtypeStruct((count * width, width), jnp.bfloat16),
        ),
        in_specs=[SMEM, VMEM, VMEM, VMEM],
        out_specs=(VMEM, VMEM),
        scratch_shapes=[
            pltpu.VMEM((places, 128), jnp.int32),
            pltpu.VMEM((halves, kinds, width, cells // halves), jnp.bfloat16),
            pltpu.VMEM((count * width, kinds * width), jnp.bfloat16),
            pltpu.VMEM((places, TILE), jnp.float32),
            pltpu.VMEM((halves, nr, nc, ns, own, TILE), jnp.bfloat16),
            pltpu.VMEM((halves, nr, nc, ns, own, TILE), jnp.bfloat16),
            pltpu.VMEM((8 * width, cells // halves), jnp.bfloat16),
            pltpu.VMEM((count * width, kinds * width), jnp.float32),
            *exchange_scratch(nr, nc, own),
        ],
        compiler_params=pltpu.CompilerParams(
            collective_id=0, has_side_effects=True, vmem_limit_bytes=60 << 20
        ),
    )(
        codes,
        density_blocks.reshape(count * width, width),
        basis,
        ext_potential,
    )
    return density, blocks.reshape(count, width * width)


def solution(mesh):
    split = P(AXES, None)
    return jax.shard_map(
        local,
        mesh=mesh,
        in_specs=(split, split, P(AXES), P(AXES), split, P(), split),
        out_specs=(split, split),
        check_vma=False,
    )
```

time: 90.8 us -> 76.9 us (0.85)
  Pallas kernels: 76.6 us -> 67.7 us
  local copies, waits for them, and re-layouts: 11.2 us -> 7.04 us
    pallas_call x1, Pallas kernels: 76.6 us -> 67.7 us  [local(): pl.pallas_call(functools.partial(fused_kernel, width, count), out_shape=(...]
    reshape x3 -> x1, local copies, waits for them, and re-layouts: 5.88 us -> 2.72 us  [local(): return (density, blocks.reshape(count, width * width))]
    add x5 -> x0, local copies, waits for them, and re-layouts: 1.21 us -> none  [the longest x3 0.93 us: local(): rowid = (planes * segs + block_segment[None, :]).reshape(-1)]
    add x4 -> x1, other arithmetic: 2.1 us -> 1.28 us  [local(): codes = (first * kinds + block_kinds[:, 0]) * kinds + block_kinds[:, 1]]
where the time goes in v3:
time: 76.9 us; the launch traced here: 76.7 us
  Pallas kernels  67.7 us (88%)
  local copies, waits for them, and re-layouts  7.04 us (9%)
  other arithmetic  1.28 us (2%)
    pallas_call x1, Pallas kernels, local(): pl.pallas_call(functools.partial(fused_kernel, width, count), out_shape=(...  67.7 us
    reshape x1, local copies, waits for them, and re-layouts, local(): density_blocks.reshape(count * width, width)  2.75 us
    reshape x1, local copies, waits for them, and re-layouts, local(): return (density, blocks.reshape(count, width * width))  2.72 us
    unnamed x1, local copies, waits for them, and re-layouts  1.57 us

profile of v3, /device:TPU:0, one launch (start us, length us, event | category | flops | bytes accessed | tf_op | source)
XLA Modules:
  0.0 76.7 jit_solution(13293854699740818177)
XLA Ops:
  0.6 1.3 %bitcast_add_fusion.codes_ref = s32[64]{0:T(128)} fusion(s32[64,2]{0,1:T(2,128)} %param.11, s32[64]{0:T(128)} %param.10, s32[64]{0:T(128)} %param.9, s32[64,1]{0,1:T(1,128)} %param.8), kind=kLoop, calls=%fused_computation | loop fusion | flops 512 | bytes 1536 | tf_op jit(solution)/shard_map/add | solution.py:348
  1.9 2.8 %reshape.12.blocks_ref = bf16[4096,64]{1,0:T(8,128)(2,1)} reshape(bf16[64,4096]{1,0:T(8,128)(2,1)} %param.7) | data formatting | bytes 1048576 | tf_op jit(solution)/shard_map/reshape | solution.py:378
  4.7 67.7 %shard_map.86 = (f32[8,4096]{1,0:T(8,128)}, bf16[4096,64]{1,0:T(8,128)(2,1)}) custom-call(s32[64]{0:T(128)} %bitcast_add_fusion.codes_ref, bf16[4096,64]{1,0:T(8,128)(2,1)} %reshape.12.blocks_ref, bf16[4,64,4096]{2,1,0:T(8,128)(2,1)} %basis_ref.1, f32[8,4096]{1,0:T(8,128)} %ext_ref.1), custom_call_target="tpu_custom_call" | custom-call | tf_op jit(solution)/shard_map/pallas_call | solution.py:354
  72.4 2.7 %reshape.13 = bf16[64,4096]{1,0:T(8,128)(2,1)} reshape(bf16[4096,64]{1,0:T(8,128)(2,1)} %get-tuple-element.5) | data formatting | bytes 1048576 | tf_op jit(solution)/shard_map/reshape | solution.py:382
  75.1 1.6 %copy.10 = f32[8,4096]{1,0:T(8,128)} copy(f32[8,4096]{1,0:T(8,128)} %get-tuple-element.8) | data formatting | bytes 262144

commit v4 on v3

--- a/solution.py
+++ b/solution.py
@@ -158,7 +158,9 @@
     tiles_ref,
     grid_ref,
     pots_ref,
-    weighted_ref,
+    even_ref,
+    odd_ref,
+    turned_ref,
     full_ref,
     *scratch,
 ):
@@ -210,11 +212,16 @@
             for g in range(groups):
                 lhs = wide_ref[g * group * width : (g + 1) * group * width, :]
                 half = jnp.dot(lhs, weights, preferred_element_type=jnp.float32)
+                half = half.astype(jnp.bfloat16)
                 sums = []
                 for b in range(group):
                     a = of_kind(h, lax.rem(lax.div(codes_ref[g * group + b], kinds), kinds), columns)
-                    product = a.astype(jnp.float32) * half[b * width : (b + 1) * width]
-                    sums.append(jnp.sum(product, axis=0, keepdims=True))
+                    product = a * half[b * width : (b + 1) * width]
+                    parts16 = [product[n : n + 16] for n in range(0, width, 16)]
+                    while len(parts16) > 1:
+                        parts16 = [x + y for x, y in zip(parts16[::2], parts16[1::2])]
+                    part = parts16[0]
+                    sums.append(jnp.sum(part.astype(jnp.float32), axis=0, keepdims=True))
                 row = pl.multiple_of(i * count + g * group, group)
                 tiles_ref[pl.ds(row, group), :] = jnp.concatenate(sums, axis=0)
             return carry
@@ -250,41 +257,57 @@
 
         lax.fori_loop(0, nr, one, 0)
 
+    def turn(h):
+        def one(i, carry):
+            columns = pl.ds(pl.multiple_of(i * TILE, TILE), TILE)
+            flat = halves_ref[h, :, :, columns].reshape(kinds * width, TILE)
+            turned_ref[h, columns, :] = flat.T
+            return carry
+
+        lax.fori_loop(0, CZB, one, 0)
+
+    def build(h, g, buffer):
+        for i in range(CZB):
+            rows = pl.ds(pl.multiple_of(i * count + g * group, group), group)
+            pots = tiles_ref[rows, :]
+            columns = pl.ds(i * TILE, TILE)
+            for b in range(group):
+                code = codes_ref[g * group + b]
+                a = of_kind(h, lax.rem(lax.div(code, kinds), kinds), columns)
+                row = jnp.broadcast_to(pots[b : b + 1], (16, TILE)).astype(jnp.bfloat16)
+                row = jnp.concatenate([row] * (width // 16), axis=0)
+                buffer[b * width : (b + 1) * width, i * TILE : (i + 1) * TILE] = a * row
+
+    def multiply(h, g, buffer):
+        full = jnp.dot(buffer[...], turned_ref[h], preferred_element_type=jnp.float32)
+        lines = pl.ds(pl.multiple_of(g * group * width, group * width), group * width)
+        if h > 0:
+            full = full + full_ref[lines, :]
+        if h < SEGW // TILE - 1:
+            full_ref[lines, :] = full
+            return
+        for b in range(group):
+            kind = lax.rem(codes_ref[g * group + b], kinds)
+            mine = jnp.where(lane_kind == kind, full[b * width : (b + 1) * width], 0.0)
+            picked = mine[:, :width]
+            for k in range(1, kinds):
+                picked = picked + mine[:, k * width : (k + 1) * width]
+            out_ref[pl.ds(pl.multiple_of((g * group + b) * width, width), width), :] = (
+                picked.astype(jnp.bfloat16)
+            )
+
     def integrate(h, first, last):
-        def block_group(g, carry):
-            for i in range(CZB):
-                rows = pl.ds(pl.multiple_of(i * count + g * group, group), group)
-                pots = tiles_ref[rows, :]
-                columns = pl.ds(i * TILE, TILE)
-                for b in range(group):
-                    a = of_kind(h, lax.rem(lax.div(codes_ref[g * group + b], kinds), kinds), columns)
-                    row = jnp.broadcast_to(pots[b : b + 1], (width, TILE)).astype(jnp.bfloat16)
-                    weighted_ref[b * width : (b + 1) * width, i * TILE : (i + 1) * TILE] = a * row
-            full = lax.dot_general(
-                weighted_ref[...],
-                halves_ref[h].reshape(kinds * width, CZB * TILE),
-                (((1,), (1,)), ((), ())),
-                preferred_element_type=jnp.float32,
-            )
-            lines = pl.ds(pl.multiple_of(g * group * width, group * width), group * width)
-            if h < SEGW // TILE - 1:
-                if h > 0:
-                    full = full + full_ref[lines, :]
-                full_ref[lines, :] = full
-                return carry
-            full = full + full_ref[lines, :]
-            for b in range(group):
-                kind = lax.rem(codes_ref[g * group + b], kinds)
-                mine = jnp.where(lane_kind == kind, full[b * width : (b + 1) * width], 0.0)
-                picked = mine[:, :width]
-                for k in range(1, kinds):
-                    picked = picked + mine[:, k * width : (k + 1) * width]
-                out_ref[pl.ds(pl.multiple_of((g * group + b) * width, width), width), :] = (
-                    picked.astype(jnp.bfloat16)
-                )
+        def pair(n, carry):
+            g = 2 * n
+            multiply(h, g, even_ref)
+            build(h, g + 1, odd_ref)
+            multiply(h, g + 1, odd_ref)
+            build(h, jnp.minimum(g + 2, groups - 2), even_ref)
             return carry
 
-        lax.fori_loop(first, last, block_group, 0)
+        if first == 0:
+            build(h, 0, even_ref)
+        lax.fori_loop(first // 2, last // 2, pair, 0)
 
     parts = []
     for h in range(SEGW // TILE):
@@ -320,18 +343,20 @@
     settle(0)
     for p in range(nr):
         late.reduce_cols(p)
-    early.pass_cols()
+    turn(0)
+    turn(1)
     for p in range(nr):
         late.reduce_rows(p)
+    early.pass_cols()
+    settle(1)
     early.pass_slab()
-    settle(1)
     early.wait()
     gather(0)
     integrate(0, 0, groups // 4)
     late.pass_cols()
-    integrate(0, groups // 4, 5 * groups // 8)
+    integrate(0, groups // 4, 3 * groups // 4)
     late.pass_slab()
-    integrate(0, 5 * groups // 8, groups)
+    integrate(0, 3 * groups // 4, groups)
     late.wait()
     gather(1)
     integrate(1, 0, groups)
@@ -367,6 +392,8 @@
             pltpu.VMEM((halves, nr, nc, ns, own, TILE), jnp.bfloat16),
             pltpu.VMEM((halves, nr, nc, ns, own, TILE), jnp.bfloat16),
             pltpu.VMEM((8 * width, cells // halves), jnp.bfloat16),
+            pltpu.VMEM((8 * width, cells // halves), jnp.bfloat16),
+            pltpu.VMEM((halves, cells // halves, kinds * width), jnp.bfloat16),
             pltpu.VMEM((count * width, kinds * width), jnp.float32),
             *exchange_scratch(nr, nc, own),
         ],

time: 76.9 us -> 78.3 us (1.018)
  Pallas kernels: 67.7 us -> 69.1 us
    pallas_call x1, Pallas kernels: 67.7 us -> 69.1 us  [local(): pl.pallas_call(functools.partial(fused_kernel, width, count), out_shape=(...]
where the time goes in v4:
time: 78.3 us; the launch traced here: 78.1 us
  Pallas kernels  69.1 us (88%)
  local copies, waits for them, and re-layouts  7.04 us (9%)
  other arithmetic  1.28 us (2%)
    pallas_call x1, Pallas kernels, local(): pl.pallas_call(functools.partial(fused_kernel, width, count), out_shape=(...  69.1 us
    reshape x1, local copies, waits for them, and re-layouts, local(): density_blocks.reshape(count * width, width)  2.75 us
    reshape x1, local copies, waits for them, and re-layouts, local(): return (density, blocks.reshape(count, width * width))  2.72 us
    unnamed x1, local copies, waits for them, and re-layouts  1.57 us

profile of v4, /device:TPU:0, one launch (start us, length us, event | category | flops | bytes accessed | tf_op | source)
XLA Modules:
  0.0 78.1 jit_solution(2595130798849569996)
XLA Ops:
  0.6 1.3 %bitcast_add_fusion.codes_ref = s32[64]{0:T(128)} fusion(s32[64,2]{0,1:T(2,128)} %param.11, s32[64]{0:T(128)} %param.10, s32[64]{0:T(128)} %param.9, s32[64,1]{0,1:T(1,128)} %param.8), kind=kLoop, calls=%fused_computation | loop fusion | flops 512 | bytes 1536 | tf_op jit(solution)/shard_map/add | solution.py:373
  1.9 2.8 %reshape.12.blocks_ref = bf16[4096,64]{1,0:T(8,128)(2,1)} reshape(bf16[64,4096]{1,0:T(8,128)(2,1)} %param.7) | data formatting | bytes 1048576 | tf_op jit(solution)/shard_map/reshape | solution.py:405
  4.7 69.1 %shard_map.86 = (f32[8,4096]{1,0:T(8,128)}, bf16[4096,64]{1,0:T(8,128)(2,1)}) custom-call(s32[64]{0:T(128)} %bitcast_add_fusion.codes_ref, bf16[4096,64]{1,0:T(8,128)(2,1)} %reshape.12.blocks_ref, bf16[4,64,4096]{2,1,0:T(8,128)(2,1)} %basis_ref.1, f32[8,4096]{1,0:T(8,128)} %ext_ref.1), custom_call_target="tpu_custom_call" | custom-call | tf_op jit(solution)/shard_map/pallas_call | solution.py:379
  73.8 2.7 %reshape.13 = bf16[64,4096]{1,0:T(8,128)(2,1)} reshape(bf16[4096,64]{1,0:T(8,128)(2,1)} %get-tuple-element.5) | data formatting | bytes 1048576 | tf_op jit(solution)/shard_map/reshape | solution.py:409
  76.5 1.6 %copy.10 = f32[8,4096]{1,0:T(8,128)} copy(f32[8,4096]{1,0:T(8,128)} %get-tuple-element.8) | data formatting | bytes 262144

commit v5 on v4

--- a/solution.py
+++ b/solution.py
@@ -343,13 +343,13 @@
     settle(0)
     for p in range(nr):
         late.reduce_cols(p)
+    early.pass_cols()
     turn(0)
     turn(1)
     for p in range(nr):
         late.reduce_rows(p)
-    early.pass_cols()
+    early.pass_slab()
     settle(1)
-    early.pass_slab()
     early.wait()
     gather(0)
     integrate(0, 0, groups // 4)

time: 78.3 us -> 75.7 us (0.967)
  Pallas kernels: 69.1 us -> 66.6 us
    pallas_call x1, Pallas kernels: 69.1 us -> 66.6 us  [local(): pl.pallas_call(functools.partial(fused_kernel, width, count), out_shape=(...]
where the time goes in v5:
time: 75.7 us; the launch traced here: 75.5 us
  Pallas kernels  66.6 us (88%)
  local copies, waits for them, and re-layouts  7.04 us (9%)
  other arithmetic  1.28 us (2%)
    pallas_call x1, Pallas kernels, local(): pl.pallas_call(functools.partial(fused_kernel, width, count), out_shape=(...  66.6 us
    reshape x1, local copies, waits for them, and re-layouts, local(): density_blocks.reshape(count * width, width)  2.75 us
    reshape x1, local copies, waits for them, and re-layouts, local(): return (density, blocks.reshape(count, width * width))  2.72 us
    unnamed x1, local copies, waits for them, and re-layouts  1.57 us

profile of v5, /device:TPU:0, one launch (start us, length us, event | category | flops | bytes accessed | tf_op | source)
XLA Modules:
  0.0 75.5 jit_solution(17919695709083370385)
XLA Ops:
  0.6 1.3 %bitcast_add_fusion.codes_ref = s32[64]{0:T(128)} fusion(s32[64,2]{0,1:T(2,128)} %param.11, s32[64]{0:T(128)} %param.10, s32[64]{0:T(128)} %param.9, s32[64,1]{0,1:T(1,128)} %param.8), kind=kLoop, calls=%fused_computation | loop fusion | flops 512 | bytes 1536 | tf_op jit(solution)/shard_map/add | solution.py:373
  1.9 2.8 %reshape.12.blocks_ref = bf16[4096,64]{1,0:T(8,128)(2,1)} reshape(bf16[64,4096]{1,0:T(8,128)(2,1)} %param.7) | data formatting | bytes 1048576 | tf_op jit(solution)/shard_map/reshape | solution.py:405
  4.7 66.6 %shard_map.86 = (f32[8,4096]{1,0:T(8,128)}, bf16[4096,64]{1,0:T(8,128)(2,1)}) custom-call(s32[64]{0:T(128)} %bitcast_add_fusion.codes_ref, bf16[4096,64]{1,0:T(8,128)(2,1)} %reshape.12.blocks_ref, bf16[4,64,4096]{2,1,0:T(8,128)(2,1)} %basis_ref.1, f32[8,4096]{1,0:T(8,128)} %ext_ref.1), custom_call_target="tpu_custom_call" | custom-call | tf_op jit(solution)/shard_map/pallas_call | solution.py:379
  71.3 2.7 %reshape.13 = bf16[64,4096]{1,0:T(8,128)(2,1)} reshape(bf16[4096,64]{1,0:T(8,128)(2,1)} %get-tuple-element.5) | data formatting | bytes 1048576 | tf_op jit(solution)/shard_map/reshape | solution.py:409
  74.0 1.6 %copy.10 = f32[8,4096]{1,0:T(8,128)} copy(f32[8,4096]{1,0:T(8,128)} %get-tuple-element.8) | data formatting | bytes 262144
